TPU v7x, 256 devices: a whole 4x4x8 slice. The times are simulated.
256 devices in a mesh: prow: 8 (over y, core), pcol: 32 (over x, z).
Axes of the slice: x: 4, y: 4, z: 8, core: 2. Of those that a mesh axis runs over, the one named last changes fastest.
Arguments:
- matrix: bfloat16 [28672, 16384], P('prow', 'pcol'), may hold values from -6 to 6
- u_inverse: float32 [2, 512, 512], replicated, may hold values from -0.02 to 0.2, as said below
- l_inverse: float32 [2, 512, 512], replicated, may hold values from -0.02 to 0.2, as said below
Outputs:
- factored: bfloat16 [28672, 16384], P('prow', 'pcol')
Inputs may be any that keep to these rules, and one draw needn't show every extreme that they name: u_inverse[p] is upper triangular with positive diagonal. l_inverse[p] is lower triangular with positive diagonal.
All inputs are finite; a program needn't handle non-finite values.
Results may differ from a plain program's by a relative error of at most 0.008.
Values may be sent and summed in bfloat16 or wider, within the bound.
No kernel may reach another device: no remote copies, remote signals or barrier semaphores. Data moves between devices by JAX's collectives and lax.ppermute only.
A program may use at most 64 MiB of HBM per device.

v0:
```python
import jax
import jax.numpy as jnp
from jax import lax
from jax.sharding import PartitionSpec as P


def broadcast(block, axis, holder):
    block = jnp.where(lax.axis_index(axis) == holder, block, jnp.zeros_like(block))
    return lax.psum(block, axis)


def body(matrix, u_inverse, l_inverse):
    width = matrix.shape[1]
    prow_index = lax.axis_index("prow")
    pcol_index = lax.axis_index("pcol")
    row_ids = jnp.arange(matrix.shape[0]) // width * lax.axis_size("prow") + prow_index
    current = matrix
    for panel_id in range(u_inverse.shape[0]):
        panel = current.astype(jnp.float32)
        lower_lower = jnp.dot(panel, u_inverse[panel_id], precision=lax.Precision.HIGHEST).astype(
            jnp.bfloat16
        )
        lower_lower = broadcast(lower_lower, "pcol", panel_id)
        lower = jnp.where(row_ids[:, None] > panel_id, lower_lower, jnp.zeros_like(lower_lower))
        upper_upper = jnp.dot(
            l_inverse[panel_id],
            current[:width].astype(jnp.float32),
            precision=lax.Precision.HIGHEST,
        ).astype(jnp.bfloat16)
        upper_upper = broadcast(upper_upper, "prow", panel_id)
        upper = jnp.where(pcol_index > panel_id, upper_upper, jnp.zeros_like(upper_upper))
        product = jnp.dot(lower, upper, preferred_element_type=jnp.float32)
        fresh = (current.astype(jnp.float32) - product).astype(jnp.bfloat16)
        keep_lower = (row_ids[:, None] > panel_id) & (pcol_index == panel_id)
        current = jnp.where(keep_lower, lower, fresh)
        current = current.at[:width].set(
            jnp.where((prow_index == panel_id) & (pcol_index > panel_id), upper, current[:width])
        )
    return current


def solution(mesh):
    in_specs = (P("prow", "pcol"), P(), P())
    out_specs = P("prow", "pcol")
    return jax.shard_map(body, mesh=mesh, in_specs=in_specs, out_specs=out_specs, check_vma=False)
```

profile of v0, /device:TPU:8, one launch (start us, length us, event | category | flops | bytes accessed | tf_op | source)
XLA Modules:
  0.0 499.8 jit_solution(11180497193374453326)
XLA Ops:
  6.5 0.0 all-reduce.7.cloned.1.call-start
  6.5 3.2 fusion.10
  9.7 0.0 all-reduce.7.cloned.1.call-update
  9.7 0.0 all-reduce.5.cloned.1.call-start
  9.8 9.2 %fusion.2 = bf16[3584,512]{1,0:T(8,128)(2,1)} fusion(bf16[3584,512]{1,0:T(8,128)(2,1)} %param.7, pred[]{:T(512)S(6)} %eq.17, f32[2,512,512]{2,1,0:T(8,128)} %param.8), kind=kOutput, calls=%fused_computation.6 | convolution fusion | flops 11277959168 | bytes 8388609 | tf_op jit(solution)/shard_map/dot_general | solution.py:20
  19.0 0.0 all-reduce.5.cloned.1.call-update
  19.0 0.0 all-reduce.11.cloned.1.call-start
  19.1 57.3 %all-reduce.7.cloned.1.call-done = bf16[512,512]{1,0:T(8,128)(2,1)} async-done(((bf16[512,512]{1,0:T(8,128)(2,1)}), bf16[512,512]{1,0:T(8,128)(2,1)}) %all-reduce.7.cloned.1.call-update) | async-done | bytes 524304 | tf_op jit(solution)/shard_map/psum | solution.py:9
  76.4 166.3 %all-reduce.5.cloned.1.call-done = bf16[3584,512]{1,0:T(8,128)(2,1)} async-done(((bf16[3584,512]{1,0:T(8,128)(2,1)}), bf16[3584,512]{1,0:T(8,128)(2,1)}) %all-reduce.5.cloned.1.call-update) | async-done | bytes 3670032 | tf_op jit(solution)/shard_map/psum | solution.py:9
  242.7 0.0 copy-start
  242.7 0.0 copy-start.2
  242.7 8.2 %fusion = bf16[3584,512]{1,0:T(8,128)(2,1)S(1)} fusion(bf16[3584,512]{1,0:T(8,128)(2,1)} %param.7, bf16[3584,512]{1,0:T(8,128)(2,1)} %all-reduce.5.cloned.1.call-done, pred[3584]{0:T(1024)(128)(4,1)S(1)} %get-tuple-element.29, pred[3584]{0:T(1024)(128)(4,1)S(1)} %get-tuple-element.30, bf16[512,512]{1,0:T(8,128)(2,1)} %all-reduce.7.cloned.1.call-done, ...), kind=kOutput, calls=%fused_computation.4 | convolution fusion | flops 1890320384 | bytes 11541505 | tf_op jit(solution)/shard_map/dot_general | solution.py:32
  250.9 0.0 copy-start.1
  250.9 1.8 copy-done.1
  252.7 0.0 copy-done
  252.7 0.0 copy-done.2
  252.7 0.0 copy-start.3
  252.7 2.1 fusion.12
  254.8 0.0 all-reduce.11.cloned.1.call-update
  254.9 0.2 all-reduce.9.cloned.1.call-start
  255.1 2.0 fusion.25
  257.1 0.0 copy-done.3
  257.1 9.5 %fusion.3 = bf16[3584,512]{1,0:T(8,128)(2,1)} fusion(bf16[3584,512]{1,0:T(8,128)(2,1)} %fusion.25, pred[]{:T(512)S(6)} %eq.16, f32[2,512,512]{2,1,0:T(8,128)S(1)} %copy-done.3), kind=kOutput, calls=%fused_computation.7 | convolution fusion | flops 11277959168 | bytes 8388609 | tf_op jit(solution)/shard_map/dot_general | solution.py:20
  266.6 0.0 all-reduce.9.cloned.1.call-update
  266.6 49.3 %all-reduce.11.cloned.1.call-done = bf16[512,512]{0,1:T(8,128)(2,1)} async-done(((bf16[512,512]{0,1:T(8,128)(2,1)}), bf16[512,512]{0,1:T(8,128)(2,1)}) %all-reduce.11.cloned.1.call-update) | async-done | bytes 524304 | tf_op jit(solution)/shard_map/psum | solution.py:9
  315.9 1.3 copy.4
  317.2 164.5 %all-reduce.9.cloned.1.call-done = bf16[3584,512]{1,0:T(8,128)(2,1)} async-done(((bf16[3584,512]{1,0:T(8,128)(2,1)}), bf16[3584,512]{1,0:T(8,128)(2,1)}) %all-reduce.9.cloned.1.call-update) | async-done | bytes 3670032 | tf_op jit(solution)/shard_map/psum | solution.py:9
  481.7 9.6 %fusion.1 = bf16[3584,512]{1,0:T(8,128)(2,1)} fusion(bf16[3584,512]{1,0:T(8,128)(2,1)} %fusion.25, bf16[3584,512]{1,0:T(8,128)(2,1)} %all-reduce.9.cloned.1.call-done, pred[3584]{0:T(1024)(128)(4,1)S(1)} %get-tuple-element.31, pred[3584]{0:T(1024)(128)(4,1)S(1)} %get-tuple-element.32, bf16[512,512]{1,0:T(8,128)(2,1)S(1)} %copy.4, pred[]{:T(512)S(6)} %gt.35), kind=kOutput, calls=%fused_computation.5 | convolution fusion | flops 1890320384 | bytes 11541505 | tf_op jit(solution)/shard_map/dot_general | solution.py:32
  491.3 2.0 fusion.21
  (2 shorter events, 0.0 us)
Async XLA Ops:
  6.5 69.8 %all-reduce.7.cloned.1.call-start = ((), (), s32[]{:S(2)}) async-start(), calls=%async_computation.1 | async-start | bytes 1048576 | tf_op jit(solution)/shard_map/psum | solution.py:9
  9.7 233.0 %all-reduce.5.cloned.1.call-start = ((), (), s32[]{:S(2)}) async-start(), calls=%async_computation | async-start | bytes 7340032 | tf_op jit(solution)/shard_map/psum | solution.py:9
  19.0 296.9 %all-reduce.11.cloned.1.call-start = ((), (), s32[]{:S(2)}) async-start(), calls=%async_computation.3 | async-start | bytes 1048576 | tf_op jit(solution)/shard_map/psum | solution.py:9
  242.7 10.0 %copy-start = (bf16[512,512]{1,0:T(8,128)(2,1)S(1)}, bf16[512,512]{1,0:T(8,128)(2,1)}, u32[]{:S(2)}) copy-start(bf16[512,512]{1,0:T(8,128)(2,1)} %all-reduce.7.cloned.1.call-done) | copy-start | bytes 1572868
  242.7 10.0 %copy-start.2 = (f32[2,512,512]{2,1,0:T(8,128)S(1)}, f32[2,512,512]{2,1,0:T(8,128)}, u32[]{:S(2)}) copy-start(f32[2,512,512]{2,1,0:T(8,128)} %param.9) | copy-start | bytes 6291460
  250.9 1.8 copy-start.1
  252.7 4.3 copy-start.3
  254.9 226.8 %all-reduce.9.cloned.1.call-start = ((), (), s32[]{:S(2)}) async-start(), calls=%async_computation.2 | async-start | bytes 7340032 | tf_op jit(solution)/shard_map/psum | solution.py:9
Sparse Core Ops, SparseCore 0:
  9.8 66.5 all-reduce.6
  80.4 162.2 all-reduce.4
  255.0 60.9 all-reduce.10
  319.4 162.2 all-reduce.8
where the time goes:
time: 500 us
  waiting for transfers between devices  437 us (87%)
  matrix products  41.7 us (8%)
  between operations  13.2 us (3%)
    psum x4, waiting for transfers between devices, broadcast(): return lax.psum(block, axis)  437 us
    dot_general x2, matrix products, body(): jnp.dot(panel, u_inverse[panel_id], precision=lax.Precision.HIGHEST)  18.7 us
    dot_general x2, matrix products, body(): product = jnp.dot(lower, upper, preferred_element_type=jnp.float32)  17.8 us
  transfers between devices with their start and end apart: 4, of which 4 were waited for; matrix products, arithmetic and copies ran while one was open for 4% of the time, Pallas kernels for 0%

commit v1 on v0

v1 whole, which is shorter than its diff:
```python
import functools

import jax
import jax.numpy as jnp
from jax import lax
from jax.experimental import pallas as pl
from jax.experimental.pallas import tpu as pltpu
from jax.sharding import PartitionSpec as P

NX, NZ = 4, 8
NB = 512
N = 224


def node(x, z):
    return (x % NX) * NZ + z % NZ


def shift(dx, dz):
    return [(node(x, z), node(x + dx, z + dz)) for x in range(NX) for z in range(NZ)]


def from_sources(x, k):
    return [(node(0, 0), node(x, -k)), (node(0, 1), node(x, 1 + k))]


def move(value, pairs):
    return lax.ppermute(value, "pcol", pairs)


def tie(*values):
    return lax.optimization_barrier(values)


def first_row(parity, k, half):
    return 2 * N * k + N * half if parity == 0 else 8 * N + 4 * N * half + N * k


def beside_y(own):
    y = lax.axis_index("prow") // 2
    ahead = lax.ppermute(own, "prow", [(0, 2), (1, 3)])
    back = lax.ppermute(own, "prow", [(0, 6), (1, 7)])
    return jnp.where(y == 1, ahead, jnp.where(y == 3, back, own))


def across_y(own):
    y = lax.axis_index("prow") // 2
    half = own.shape[0] // 2
    low = lax.ppermute(own[:half], "prow", [(2, 4), (3, 5)])
    high = lax.ppermute(own[half:], "prow", [(6, 4), (7, 5)])
    return jnp.where(y == 2, jnp.concatenate([low, high], 0), own)


def swap_cores(value):
    return lax.ppermute(value, "prow", [(i, i ^ 1) for i in range(8)])


def grow(value, stage, x, z, core):
    def send(hops):
        pairs = [
            (NX * NZ * prow + node(a[0], a[1] + 1 - prow), NX * NZ * prow + node(b[0], b[1] + 1 - prow))
            for prow in (0, 1)
            for a, b in hops
        ]
        return lax.ppermute(value, ("prow", "pcol"), pairs)

    c = (z - 1 + core + NZ) % NZ
    if stage == 0:
        two, six, four = (send([((0, 0), (0, d))]) for d in (2, 6, 4))
        there = jnp.where(c == 2, two, jnp.where(c == 6, six, four))
        return jnp.where((x == 0) & (c % 2 == 0) & (c > 0), there, value)
    if stage == 1:
        one, three, two = (send([((0, d), (r, d)) for d in (0, 2, 4, 6)]) for r in (1, 3, 2))
        there = jnp.where(x == 1, one, jnp.where(x == 3, three, two))
        return jnp.where((x > 0) & (c % 2 == 0), there, value)
    return jnp.where(c % 2 == 1, send([((r, d), (r, d + 1)) for r in range(NX) for d in (0, 2, 4, 6)]), value)


def exchange(matrix, x, z, k, core, make_weights):
    block = matrix[:NB]
    parts = tie(*[matrix[2 * N * kk : 2 * N * (kk + 1)] for kk in (1, 2, 3)], matrix)
    even = [move(parts[kk - 1], from_sources(0, kk)) for kk in (1, 2, 3)]
    one = move(parts[3][8 * N : 12 * N], from_sources(1, 0))
    three = move(parts[3][12 * N : 16 * N], from_sources(3, 0))

    def along(value, kk):
        return move(value, [p for r in (1, 3) for p in ((node(r, 0), node(r, -kk)), (node(r, 1), node(r, 1 + kk)))])

    one, three, *even = tie(one, three, *even)
    held = jnp.where(x == 1, one, three)
    odd = [along(held[N * kk : N * (kk + 1)], kk) for kk in (1, 2, 3)]
    extra = grow(block, 0, x, z, core)

    def choose(own, one, two, three):
        return jnp.where(k == 0, own, jnp.where(k == 1, one, jnp.where(k == 2, two, three)))

    single = choose(held[:N], *odd)
    both = choose(matrix[: 2 * N], *even)
    sent = jnp.where(x == 0, both, jnp.concatenate([single, single], 0))
    sent, extra = tie(sent, extra)
    came = move(sent, [(node(a, c), node(b, c)) for a, b in ((0, 2), (1, 3), (3, 1)) for c in range(NZ)])
    extra = grow(extra, 1, x, z, core)
    first = jnp.where(x == 3, came[:N], sent[:N])
    second = jnp.where(x == 1, came[:N], sent[N:])
    double = jnp.where(x == 2, came, jnp.concatenate([first, second], 0))

    double, extra = tie(double, extra)
    near_rows, far_rows = [(double, 0, 0, 0, 2)], []
    up = down = double
    xup, xdown = double[:N], double[N:]
    carried = (extra,)
    for s in range(1, 5):
        if s == 4:
            up, down = up[:N], down[N:]
        dz = s - 1
        up, down = move(up, shift(0, 1)), move(down, shift(0, -1))
        xup, xdown = move(xup, shift(1, 0)), move(xdown, shift(-1, 0))
        if s == 1:
            carried = (jnp.concatenate([block, grow(carried[0], 2, x, z, core)], 0),)
        elif s == 2:
            carried = make_weights(carried[0], swap_cores(carried[0]))
        elif s == 3:
            carried = (beside_y(carried[0]), carried[1])
        else:
            carried = (across_y(carried[0]), carried[1])
        up, down, xup, xdown, *carried = tie(up, down, xup, xdown, *carried)
        whole = 2 if 1 < s else 1
        far_rows.append((xup, 1, -dz, 0, whole))
        far_rows.append((xdown, 1, dz, 1 if s == 1 else 0, whole))
        near_rows.append((up, 0, -s, 0, 2 if s < 4 else 1))
        near_rows.append((down, 0, s, 0 if s < 4 else 1, 2 if s < 4 else 1))
        xup, xdown = up, down
    far_rows.append((move(xup, shift(1, 0)), 1, -4, 0, 1))
    far_rows.append((move(xdown, shift(-1, 0)), 1, 4, 1, 1))
    weights, top = carried
    return near_rows, far_rows, (weights, swap_cores(weights)), top


def dot(a, b):
    return jnp.dot(a, b, preferred_element_type=jnp.float32)


def split(value):
    big = value * 65537.0
    high = big - (big - value)
    return high.astype(jnp.bfloat16), (value - high).astype(jnp.bfloat16)


def accurate(a, b):
    if isinstance(a, tuple) and isinstance(b, tuple):
        return dot(a[0], b[0]) + dot(a[0], b[1]) + dot(a[1], b[0])
    if isinstance(a, tuple):
        return dot(a[0], b) + dot(a[1], b)
    return dot(a, b[0]) + dot(a, b[1])


def weights_kernel(ids, mine, other, u, l, weights, top):
    prow, pcol = ids[0], ids[1]
    even = prow % 2 == 0
    head0, right = jnp.where(even, mine[:NB], other[:NB]), jnp.where(even, mine[NB:], other[NB:])
    head1, below = jnp.where(even, other[:NB], mine[:NB]), jnp.where(even, other[NB:], mine[NB:])
    u0, u1, l0, l1 = split(u[0]), split(u[1]), split(l[0]), split(l[1])
    upper01 = accurate(l0, right).astype(jnp.bfloat16)
    upper0 = accurate(l0, head0).astype(jnp.bfloat16)
    lower = accurate(below, u0).astype(jnp.bfloat16)
    step = jnp.where(pcol > 0, dot(lower, upper0), 0.0)
    fresh = (head1.astype(jnp.float32) - step).astype(jnp.bfloat16)
    upper1 = accurate(l1, fresh).astype(jnp.bfloat16)
    second = jnp.where(pcol > 1, accurate(u1, upper1), jnp.where(pcol == 1, -u[1], 0.0))
    row = lax.broadcasted_iota(jnp.int32, (NB, NB), 0)
    col = lax.broadcasted_iota(jnp.int32, (NB, NB), 1)
    minus_one = jnp.where((row == col) & (pcol == 0), -1.0, 0.0)
    base = jnp.where(pcol > 1, upper0.astype(jnp.float32), minus_one)
    first = accurate(u0, split(base - accurate(upper01, split(second))))
    weights[...] = jnp.where(even, first, second).astype(jnp.bfloat16)
    top0 = jnp.where(pcol > 0, upper0, head0)
    top1 = jnp.where(pcol > 1, upper1, jnp.where(pcol == 1, fresh, lower))
    top[...] = jnp.where(prow == 0, top0, top1)


def make_weights(ids, heads, others, u_inverse, l_inverse):
    vmem = pl.BlockSpec(memory_space=pltpu.VMEM)
    return pl.pallas_call(
        weights_kernel,
        out_shape=(
            jax.ShapeDtypeStruct((NB, NB), jnp.bfloat16),
            jax.ShapeDtypeStruct((NB, NB), jnp.bfloat16),
        ),
        in_specs=[pl.BlockSpec(memory_space=pltpu.SMEM)] + [vmem] * 4,
        out_specs=(vmem, vmem),
        compiler_params=pltpu.CompilerParams(vmem_limit_bytes=48 * 1024 * 1024),
        cost_estimate=pl.CostEstimate(flops=34 * NB**3, bytes_accessed=16 * NB * NB, transcendentals=0),
    )(ids, heads, others, u_inverse, l_inverse)


def factor_kernel(plan, part, ids, a_hbm, mine_hbm, other_hbm, top_hbm, *refs):
    count = len(plan)
    bufs, out_hbm = refs[:count], refs[-8]
    panels, a, out, w, top, sems, out_sems = refs[-7:]
    prow, pcol = ids[0], ids[1]
    x, z = pcol // NZ, pcol % NZ
    parity = (x + part) % 2
    rows = a.shape[0]
    base = pl.multiple_of(parity * rows, 16)
    slots = 16
    copies = []

    def start(src, dst):
        copy = pltpu.make_async_copy(src, dst, sems.at[slots + len(copies)])
        copy.start()
        copies.append(copy)

    core = prow % 2
    start(mine_hbm, w.at[pl.ds(pl.multiple_of(core * NB, NB), NB)])
    start(other_hbm, w.at[pl.ds(pl.multiple_of((1 - core) * NB, NB), NB)])
    start(a_hbm.at[pl.ds(base, rows)], a)
    start(top_hbm, top)

    def landing(panel, k, half):
        at = jnp.where(parity == 0, first_row(0, k, half), first_row(1, k, half) - rows)
        return panels.at[panel, pl.ds(pl.multiple_of(at, 16), N)], sems.at[8 * panel + 2 * k + half]

    for buf, (_, dz, first, halves) in zip(bufs, plan):
        zz = (z + dz + NZ) % NZ
        panel = jnp.where((zz >= 1) & (zz <= 4), 1, 0)
        k = jnp.where(panel == 1, zz - 1, (NZ - zz) % NZ)
        for i in range(halves):
            dst, sem = landing(panel, k, first + i)
            pltpu.make_async_copy(buf.at[pl.ds(i * N, N)], dst, sem).start()
    for copy in copies:
        copy.wait()
    size = 2 * N
    for s in range(rows // size):
        at = pl.ds(s * size, size)
        for panel in range(2):
            for i in range(2):
                k = jnp.where(parity == 0, s, 2 * (s % 2) + i)
                half = jnp.where(parity == 0, i, s // 2)
                dst, sem = landing(panel, k, half)
                pltpu.make_async_copy(bufs[0].at[pl.ds(0, N)], dst, sem).wait()
        product = dot(panels[0, at], w[:NB]) + dot(panels[1, at], w[NB:])
        value = jnp.where(pcol > 1, a[at].astype(jnp.float32), 0.0)
        out[at] = (value - product).astype(jnp.bfloat16)
        if s == 0:

            @pl.when((parity == 0) & (prow < 2))
            def _():
                out[:size] = top[:size]

        if s == 1:

            @pl.when((parity == 0) & (prow < 2))
            def _():
                out[size:NB] = top[size:]

        to = pl.ds(pl.multiple_of(base + s * size, 16), size)
        pltpu.make_async_copy(out.at[at], out_hbm.at[to], out_sems.at[s]).start()
    for s in range(rows // size):
        at = pl.ds(s * size, size)
        to = pl.ds(pl.multiple_of(base + s * size, 16), size)
        pltpu.make_async_copy(out.at[at], out_hbm.at[to], out_sems.at[s]).wait()


def factor(part, ids, matrix, weights, top, got, result=None):
    rows = matrix.shape[0] // 2
    plan = tuple(entry[1:] for entry in got)
    operands = [ids, matrix, *weights, top] + [entry[0] for entry in got] + ([] if result is None else [result])
    hbm = pl.BlockSpec(memory_space=pl.ANY)
    return pl.pallas_call(
        functools.partial(factor_kernel, plan, part),
        out_shape=jax.ShapeDtypeStruct(matrix.shape, matrix.dtype),
        in_specs=[pl.BlockSpec(memory_space=pltpu.SMEM)] + [hbm] * (len(operands) - 1),
        out_specs=hbm,
        input_output_aliases={} if result is None else {len(operands) - 1: 0},
        scratch_shapes=[
            pltpu.VMEM((2, rows, NB), jnp.bfloat16),
            pltpu.VMEM((rows, NB), jnp.bfloat16),
            pltpu.VMEM((rows, NB), jnp.bfloat16),
            pltpu.VMEM((2 * NB, NB), jnp.bfloat16),
            pltpu.VMEM((NB, NB), jnp.bfloat16),
            pltpu.SemaphoreType.DMA((20,)),
            pltpu.SemaphoreType.DMA((rows // (2 * N),)),
        ],
        compiler_params=pltpu.CompilerParams(vmem_limit_bytes=56 * 1024 * 1024),
        cost_estimate=pl.CostEstimate(flops=4 * rows * NB * NB, bytes_accessed=8 * rows * NB, transcendentals=0),
    )(*operands)


def body(matrix, u_inverse, l_inverse):
    prow, pcol = lax.axis_index("prow"), lax.axis_index("pcol")
    x, z = pcol // NZ, pcol % NZ
    k = jnp.where((z >= 1) & (z <= 4), z - 1, (NZ - z) % NZ)
    ids = jnp.stack([prow, pcol]).astype(jnp.int32)
    near_rows, far_rows, weights, top = exchange(
        matrix, x, z, k, prow % 2, lambda mine, other: make_weights(ids, mine, other, u_inverse, l_inverse)
    )
    half = factor(0, ids, matrix, weights, top, near_rows)
    return factor(1, ids, matrix, weights, top, far_rows, half)


def solution(mesh):
    in_specs = (P("prow", "pcol"), P(), P())
    return jax.shard_map(body, mesh=mesh, in_specs=in_specs, out_specs=P("prow", "pcol"), check_vma=False)
```

time: 500 us -> 182 us (0.36)
  the two profiles are of different devices: /device:TPU:8 before, /device:TPU:152 now
where the time goes in v1:
time: 182 us; the launch traced here: 181 us
  waiting for transfers between devices  90.9 us (50%)
  starting transfers between devices  51.9 us (29%)
  Pallas kernels  21.1 us (12%)
  local copies, waits for them, and re-layouts  8.65 us (5%)
  other arithmetic  7.55 us (4%)
    ppermute x27, waiting for transfers between devices, move(): return lax.ppermute(value, 'pcol', pairs)  57.4 us
    ppermute x27, starting transfers between devices, move(): return lax.ppermute(value, 'pcol', pairs)  39.9 us
    ppermute x1, waiting for transfers between devices, beside_y(): back = lax.ppermute(own, 'prow', [(0, 6), (1, 7)])  33.5 us
    pallas_call x2, Pallas kernels, factor(): pl.pallas_call(functools.partial(factor_kernel, plan, part), out_shape=ja...  14.4 us
    ppermute x7, starting transfers between devices, send(): return lax.ppermute(value, ('prow', 'pcol'), pairs)  7.89 us
    pallas_call x1, Pallas kernels, make_weights(): pl.pallas_call(weights_kernel, out_shape=(jax.ShapeDtypeStruct((NB, NB),...  6.67 us
  transfers between devices with their start and end apart: 40, of which 12 were waited for; matrix products, arithmetic and copies ran while one was open for 3% of the time, Pallas kernels for 8%

profile of v1, /device:TPU:152, one launch (start us, length us, event | category | flops | bytes accessed | tf_op | source)
XLA Modules:
  0.0 180.9 jit_solution(1092890773802247875)
XLA Ops:
  0.0 2.4 %fusion.1 = (bf16[448,512]{1,0:T(8,128)(2,1)}, bf16[448,512]{1,0:T(8,128)(2,1)}, bf16[448,512]{1,0:T(8,128)(2,1)}) fusion(bf16[3584,512]{1,0:T(8,128)(2,1)} %a_hbm.3), kind=kLoop, calls=%fused_computation.14 | loop fusion | bytes 2752512 | tf_op jit(solution)/shard_map/slice | solution.py:81
  2.4 1.6 fusion
  4.7 1.7 collective-permute-start
  13.2 28.5 %collective-permute-done.4 = bf16[448,512]{1,0:T(8,128)(2,1)} collective-permute-done((bf16[448,512]{1,0:T(8,128)(2,1)}, bf16[448,512]{1,0:T(8,128)(2,1)}, u32[]{:S(2)}, u32[]{:S(2)}) %collective-permute-start.4) | collective-permute-done | bytes 458784 | tf_op jit(solution)/shard_map/ppermute | solution.py:28
  44.6 2.0 %select_select_fusion.2 = bf16[512,512]{1,0:T(8,128)(2,1)} fusion(bf16[512,512]{1,0:T(8,128)(2,1)S(1)} %collective-permute-done.8, bf16[512,512]{1,0:T(8,128)(2,1)S(1)} %collective-permute-done.9, bf16[512,512]{1,0:T(8,128)(2,1)S(1)} %collective-permute-done.10, pred[]{:T(512)S(6)} %eq.68, pred[]{:T(512)S(6)} %eq.67, pred[]{:T(512)S(6)} %and.57, ...), kind=kLoop, calls=%fused_computation.5 | loop fusion | flops 786432 | bytes 2621443 | tf_op jit(solution)/shard_map/jit(_where)/select_n | solution.py:71
  46.7 1.5 maximum_select_fusion.1
  49.5 1.5 collective-permute-start.14
  51.0 1.5 collective-permute-start.13
  52.4 1.5 collective-permute-start.12
  53.9 4.8 %collective-permute-done.11 = bf16[448,512]{1,0:T(8,128)(2,1)S(1)} collective-permute-done((bf16[448,512]{1,0:T(8,128)(2,1)S(1)}, bf16[448,512]{1,0:T(8,128)(2,1)S(1)}, u32[]{:S(2)}, u32[]{:S(2)}) %collective-permute-start.11) | collective-permute-done | bytes 458784 | tf_op jit(solution)/shard_map/ppermute | solution.py:28
  58.9 2.3 %select_select_fusion.1 = bf16[512,512]{1,0:T(8,128)(2,1)} fusion(bf16[512,512]{1,0:T(8,128)(2,1)} %select_select_fusion.2, bf16[512,512]{1,0:T(8,128)(2,1)} %collective-permute-done.12, bf16[512,512]{1,0:T(8,128)(2,1)} %collective-permute-done.13, bf16[512,512]{1,0:T(8,128)(2,1)} %collective-permute-done.14, pred[]{:T(512)S(6)} %eq.69, pred[]{:T(512)S(6)} %eq.65, ...), kind=kLoop, calls=%fused_computation.4 | loop fusion | flops 786432 | bytes 2621443 | tf_op jit(solution)/shard_map/jit(_where)/select_n | solution.py:75
  62.6 2.0 %collective-permute-start.15 = (bf16[448,512]{1,0:T(8,128)(2,1)S(1)}, bf16[448,512]{1,0:T(8,128)(2,1)S(1)}, u32[]{:S(2)}, u32[]{:S(2)}) collective-permute-start(bf16[448,512]{1,0:T(8,128)(2,1)S(1)} %maximum_select_fusion.2.refs_0_), channel_id=1, source_target_pairs={{0,1},{1,2},{2,3},{3,4},{4,5},{5,6},{6,7},{7,0},{8,9},{9,10},{10,1... | collective-permute-start | bytes 1376264 | tf_op jit(solution)/shard_map/ppermute | solution.py:28
  64.8 2.0 %collective-permute-start.17 = (bf16[224,512]{1,0:T(8,128)(2,1)S(1)}, bf16[224,512]{1,0:T(8,128)(2,1)S(1)}, u32[]{:S(2)}, u32[]{:S(2)}) collective-permute-start(bf16[224,512]{1,0:T(8,128)(2,1)S(1)} %get-tuple-element.94), channel_id=1, source_target_pairs={{0,8},{1,9},{2,10},{3,11},{4,12},{5,13},{6,14},{7,15},{8,16},{9,17... | collective-permute-start | bytes 688136 | tf_op jit(solution)/shard_map/ppermute | solution.py:28
  68.0 2.8 %collective-permute-done.18.refs_1_ = bf16[224,512]{1,0:T(8,128)(2,1)S(1)} collective-permute-done((bf16[224,512]{1,0:T(8,128)(2,1)S(1)}, bf16[224,512]{1,0:T(8,128)(2,1)S(1)}, u32[]{:S(2)}, u32[]{:S(2)}) %collective-permute-start.18) | collective-permute-done | bytes 229408 | tf_op jit(solution)/shard_map/ppermute | solution.py:28
  70.8 2.5 %collective-permute-done.17.refs_0_ = bf16[224,512]{1,0:T(8,128)(2,1)S(1)} collective-permute-done((bf16[224,512]{1,0:T(8,128)(2,1)S(1)}, bf16[224,512]{1,0:T(8,128)(2,1)S(1)}, u32[]{:S(2)}, u32[]{:S(2)}) %collective-permute-start.17) | collective-permute-done | bytes 229408 | tf_op jit(solution)/shard_map/ppermute | solution.py:28
  74.6 2.7 %collective-permute-start.22 = (bf16[448,512]{1,0:T(8,128)(2,1)S(1)}, bf16[448,512]{1,0:T(8,128)(2,1)S(1)}, u32[]{:S(2)}, u32[]{:S(2)}) collective-permute-start(bf16[448,512]{1,0:T(8,128)(2,1)S(1)} %collective-permute-done.15.refs_1_), channel_id=1, source_target_pairs={{0,8},{1,9},{2,10},{3,11},{4,12},{5,13},{6,14},{7,15},{8,16},{9,17... | collective-permute-start | bytes 1376264 | tf_op jit(solution)/shard_map/ppermute | solution.py:28
  77.3 1.9 %collective-permute-start.23 = (bf16[448,512]{1,0:T(8,128)(2,1)S(1)}, bf16[448,512]{1,0:T(8,128)(2,1)S(1)}, u32[]{:S(2)}, u32[]{:S(2)}) collective-permute-start(bf16[448,512]{1,0:T(8,128)(2,1)S(1)} %collective-permute-done.16.refs_2_), channel_id=1, source_target_pairs={{0,24},{1,25},{2,26},{3,27},{4,28},{5,29},{6,30},{7,31},{8,0},{9,1... | collective-permute-start | bytes 1376264 | tf_op jit(solution)/shard_map/ppermute | solution.py:28
  79.2 1.9 %collective-permute-start.21 = (bf16[448,512]{1,0:T(8,128)(2,1)S(1)}, bf16[448,512]{1,0:T(8,128)(2,1)}, u32[]{:S(2)}, u32[]{:S(2)}) collective-permute-start(bf16[448,512]{1,0:T(8,128)(2,1)S(1)} %collective-permute-done.16.refs_2_), channel_id=1, source_target_pairs={{0,7},{1,0},{2,1},{3,2},{4,3},{5,4},{6,5},{7,6},{8,15},{9,8},{10,9... | collective-permute-start | bytes 1376264 | tf_op jit(solution)/shard_map/ppermute | solution.py:28
  81.2 6.7 %shard_map.37 = (bf16[512,512]{1,0:T(8,128)(2,1)S(1)}, bf16[512,512]{1,0:T(8,128)(2,1)S(1)}) custom-call(s32[2]{0:T(128)S(1)} %pad_add_fusion.ids, bf16[1024,512]{1,0:T(8,128)(2,1)S(1)} %pad_maximum_fusion.mine, bf16[1024,512]{1,0:T(8,128)(2,1)S(1)} %collective-permute-done.24.other, f32[2,512,512]{2,1,0:T(8,128)S(1)} %copy-done.2, f32[2,512,512]{2,1,0:T(8,128)} %l.1), custom_call_target="tpu_custom_call" | custom-call | flops 4563402752 | bytes 4194304 | tf_op jit(solution)/shard_map/pallas_call | solution.py:183
  88.7 2.5 %collective-permute-done.20.refs_3_ = bf16[448,512]{1,0:T(8,128)(2,1)} collective-permute-done((bf16[448,512]{1,0:T(8,128)(2,1)S(1)}, bf16[448,512]{1,0:T(8,128)(2,1)}, u32[]{:S(2)}, u32[]{:S(2)}) %collective-permute-start.20) | collective-permute-done | bytes 458784 | tf_op jit(solution)/shard_map/ppermute | solution.py:28
  94.5 1.6 collective-permute-start.25
  96.1 3.1 %collective-permute-start.28 = (bf16[448,512]{1,0:T(8,128)(2,1)}, bf16[448,512]{1,0:T(8,128)(2,1)}, u32[]{:S(2)}, u32[]{:S(2)}) collective-permute-start(bf16[448,512]{1,0:T(8,128)(2,1)} %collective-permute-done.21.refs_4_), channel_id=1, source_target_pairs={{0,24},{1,25},{2,26},{3,27},{4,28},{5,29},{6,30},{7,31},{8,0},{9,1... | collective-permute-start | bytes 1376264 | tf_op jit(solution)/shard_map/ppermute | solution.py:28
  99.2 33.5 %collective-permute-done.30 = bf16[512,512]{1,0:T(8,128)(2,1)S(1)} collective-permute-done((bf16[512,512]{1,0:T(8,128)(2,1)S(1)}, bf16[512,512]{1,0:T(8,128)(2,1)S(1)}, u32[]{:S(2)}, u32[]{:S(2)}) %collective-permute-start.30) | collective-permute-done | bytes 524320 | tf_op jit(solution)/shard_map/ppermute | solution.py:42
  132.7 3.1 %collective-permute-start.26 = (bf16[448,512]{1,0:T(8,128)(2,1)}, bf16[448,512]{1,0:T(8,128)(2,1)S(1)}, u32[]{:S(2)}, u32[]{:S(2)}) collective-permute-start(bf16[448,512]{1,0:T(8,128)(2,1)} %collective-permute-done.21.refs_4_), channel_id=1, source_target_pairs={{0,7},{1,0},{2,1},{3,2},{4,3},{5,4},{6,5},{7,6},{8,15},{9,8},{10,9... | collective-permute-start | bytes 1376264 | tf_op jit(solution)/shard_map/ppermute | solution.py:28
  135.9 8.3 %collective-permute-done.26.refs_6_ = bf16[448,512]{1,0:T(8,128)(2,1)S(1)} collective-permute-done((bf16[448,512]{1,0:T(8,128)(2,1)}, bf16[448,512]{1,0:T(8,128)(2,1)S(1)}, u32[]{:S(2)}, u32[]{:S(2)}) %collective-permute-start.26) | collective-permute-done | bytes 458784 | tf_op jit(solution)/shard_map/ppermute | solution.py:28
  147.2 2.3 %collective-permute-start.34 = (bf16[448,512]{1,0:T(8,128)(2,1)S(1)}, bf16[448,512]{1,0:T(8,128)(2,1)S(1)}, u32[]{:S(2)}, u32[]{:S(2)}) collective-permute-start(bf16[448,512]{1,0:T(8,128)(2,1)S(1)} %collective-permute-done.26.refs_6_), channel_id=1, source_target_pairs={{0,24},{1,25},{2,26},{3,27},{4,28},{5,29},{6,30},{7,31},{8,0},{9,1... | collective-permute-start | bytes 1376264 | tf_op jit(solution)/shard_map/ppermute | solution.py:28
  149.5 3.7 %collective-permute-start.32 = (bf16[224,512]{1,0:T(8,128)(2,1)S(1)}, bf16[224,512]{1,0:T(8,128)(2,1)S(1)}, u32[]{:S(2)}, u32[]{:S(2)}) collective-permute-start(bf16[224,512]{1,0:T(8,128)(2,1)S(1)} %slice.78), channel_id=1, source_target_pairs={{0,7},{1,0},{2,1},{3,2},{4,3},{5,4},{6,5},{7,6},{8,15},{9,8},{10,9... | collective-permute-start | bytes 688136 | tf_op jit(solution)/shard_map/ppermute | solution.py:28
  153.4 3.4 %collective-permute-done.32.refs_8_ = bf16[224,512]{1,0:T(8,128)(2,1)S(1)} collective-permute-done((bf16[224,512]{1,0:T(8,128)(2,1)S(1)}, bf16[224,512]{1,0:T(8,128)(2,1)S(1)}, u32[]{:S(2)}, u32[]{:S(2)}) %collective-permute-start.32) | collective-permute-done | bytes 229408 | tf_op jit(solution)/shard_map/ppermute | solution.py:28
  156.7 3.7 %collective-permute-done.31.refs_7_ = bf16[224,512]{1,0:T(8,128)(2,1)S(1)} collective-permute-done((bf16[224,512]{1,0:T(8,128)(2,1)S(1)}, bf16[224,512]{1,0:T(8,128)(2,1)S(1)}, u32[]{:S(2)}, u32[]{:S(2)}) %collective-permute-start.31) | collective-permute-done | bytes 229408 | tf_op jit(solution)/shard_map/ppermute | solution.py:28
  160.9 3.2 %collective-permute-start.39 = (bf16[224,512]{1,0:T(8,128)(2,1)S(1)}, bf16[224,512]{1,0:T(8,128)(2,1)S(1)}, u32[]{:S(2)}, u32[]{:S(2)}) collective-permute-start(bf16[224,512]{1,0:T(8,128)(2,1)S(1)} %collective-permute-done.32.refs_8_), channel_id=1, source_target_pairs={{0,24},{1,25},{2,26},{3,27},{4,28},{5,29},{6,30},{7,31},{8,0},{9,1... | collective-permute-start | bytes 688136 | tf_op jit(solution)/shard_map/ppermute | solution.py:28
  164.9 7.2 %shard_map.38.refs_10_ = bf16[3584,512]{1,0:T(8,128)(2,1)} custom-call(s32[2]{0:T(128)} %copy-done.1, bf16[3584,512]{1,0:T(8,128)(2,1)} %a_hbm.3, bf16[512,512]{1,0:T(8,128)(2,1)} %copy-done.3, bf16[512,512]{1,0:T(8,128)(2,1)} %copy-done.5, bf16[512,512]{1,0:T(8,128)(2,1)} %copy-done, bf16[448,512]{1,0:T(8,128)(2,1)} %copy-done.4, ...), custom_call_target="tpu_custom_call" | custom-call | flops 1879048192 | bytes 7340032 | tf_op jit(solution)/shard_map/pallas_call | solution.py:269
  173.6 7.2 %shard_map.39 = bf16[3584,512]{1,0:T(8,128)(2,1)} custom-call(s32[2]{0:T(128)} %copy-done.1, bf16[3584,512]{1,0:T(8,128)(2,1)} %a_hbm.3, bf16[512,512]{1,0:T(8,128)(2,1)} %copy-done.3, bf16[512,512]{1,0:T(8,128)(2,1)} %copy-done.5, bf16[512,512]{1,0:T(8,128)(2,1)} %copy-done, bf16[224,512]{1,0:T(8,128)(2,1)} %copy-done.15, ...), custom_call_target="tpu_custom_call", output_to_operand_aliasing={{}: (15, {})} | custom-call | flops 1879048192 | bytes 7340032 | tf_op jit(solution)/shard_map/pallas_call | solution.py:269
  (111 shorter events, 25.9 us)
Async XLA Ops:
  4.0 38.4 %collective-permute-start.1 = (bf16[896,512]{1,0:T(8,128)(2,1)S(1)}, bf16[896,512]{1,0:T(8,128)(2,1)S(1)}, u32[]{:S(2)}, u32[]{:S(2)}) collective-permute-start(bf16[896,512]{1,0:T(8,128)(2,1)S(1)} %get-tuple-element.81), channel_id=1, source_target_pairs={{0,24},{1,25},{32,56},{33,57},{64,88},{65,89},{96,120},{97,121},{1... | collective-permute-start | bytes 2752520 | tf_op jit(solution)/shard_map/ppermute | solution.py:28
  4.7 37.7 %collective-permute-start = (bf16[896,512]{1,0:T(8,128)(2,1)S(1)}, bf16[896,512]{1,0:T(8,128)(2,1)}, u32[]{:S(2)}, u32[]{:S(2)}) collective-permute-start(bf16[896,512]{1,0:T(8,128)(2,1)S(1)} %get-tuple-element.82), channel_id=1, source_target_pairs={{0,8},{1,9},{32,40},{33,41},{64,72},{65,73},{96,104},{97,105},{128... | collective-permute-start | bytes 2752520 | tf_op jit(solution)/shard_map/ppermute | solution.py:28
  9.3 32.4 %collective-permute-start.4 = (bf16[448,512]{1,0:T(8,128)(2,1)}, bf16[448,512]{1,0:T(8,128)(2,1)}, u32[]{:S(2)}, u32[]{:S(2)}) collective-permute-start(bf16[448,512]{1,0:T(8,128)(2,1)} %get-tuple-element.46), channel_id=1, source_target_pairs={{0,5},{1,4},{32,37},{33,36},{64,69},{65,68},{96,101},{97,100},{128... | collective-permute-start | bytes 1376264 | tf_op jit(solution)/shard_map/ppermute | solution.py:28
  11.8 32.2 %collective-permute-start.10 = (bf16[512,512]{1,0:T(8,128)(2,1)S(1)}, bf16[512,512]{1,0:T(8,128)(2,1)S(1)}, u32[]{:S(2)}, u32[]{:S(2)}) collective-permute-start(bf16[512,512]{1,0:T(8,128)(2,1)S(1)} %slice.71), channel_id=1, source_target_pairs={{1,5},{32,36}} | collective-permute-start | bytes 1572872 | tf_op jit(solution)/shard_map/ppermute | solution.py:65
  12.5 32.1 %collective-permute-start.9 = (bf16[512,512]{1,0:T(8,128)(2,1)S(1)}, bf16[512,512]{1,0:T(8,128)(2,1)S(1)}, u32[]{:S(2)}, u32[]{:S(2)}) collective-permute-start(bf16[512,512]{1,0:T(8,128)(2,1)S(1)} %slice.71), channel_id=1, source_target_pairs={{1,7},{32,38}} | collective-permute-start | bytes 1572872 | tf_op jit(solution)/shard_map/ppermute | solution.py:65
  48.2 10.5 %collective-permute-start.11 = (bf16[448,512]{1,0:T(8,128)(2,1)S(1)}, bf16[448,512]{1,0:T(8,128)(2,1)S(1)}, u32[]{:S(2)}, u32[]{:S(2)}) collective-permute-start(bf16[448,512]{1,0:T(8,128)(2,1)S(1)} %maximum_select_fusion.1), channel_id=1, source_target_pairs={{0,16},{1,17},{2,18},{3,19},{4,20},{5,21},{6,22},{7,23},{8,24},{9,... | collective-permute-start | bytes 1376264 | tf_op jit(solution)/shard_map/ppermute | solution.py:28
  49.5 9.3 %collective-permute-start.14 = (bf16[512,512]{1,0:T(8,128)(2,1)}, bf16[512,512]{1,0:T(8,128)(2,1)}, u32[]{:S(2)}, u32[]{:S(2)}) collective-permute-start(bf16[512,512]{1,0:T(8,128)(2,1)} %select_select_fusion.2), channel_id=1, source_target_pairs={{1,17},{3,19},{5,21},{7,23},{32,48},{34,50},{36,52},{38,54}} | collective-permute-start | bytes 1572872 | tf_op jit(solution)/shard_map/ppermute | solution.py:65
  51.0 7.9 %collective-permute-start.13 = (bf16[512,512]{1,0:T(8,128)(2,1)}, bf16[512,512]{1,0:T(8,128)(2,1)}, u32[]{:S(2)}, u32[]{:S(2)}) collective-permute-start(bf16[512,512]{1,0:T(8,128)(2,1)} %select_select_fusion.2), channel_id=1, source_target_pairs={{1,25},{3,27},{5,29},{7,31},{32,56},{34,58},{36,60},{38,62}} | collective-permute-start | bytes 1572872 | tf_op jit(solution)/shard_map/ppermute | solution.py:65
  52.4 6.4 %collective-permute-start.12 = (bf16[512,512]{1,0:T(8,128)(2,1)}, bf16[512,512]{1,0:T(8,128)(2,1)}, u32[]{:S(2)}, u32[]{:S(2)}) collective-permute-start(bf16[512,512]{1,0:T(8,128)(2,1)} %select_select_fusion.2), channel_id=1, source_target_pairs={{1,9},{3,11},{5,13},{7,15},{32,40},{34,42},{36,44},{38,46}} | collective-permute-start | bytes 1572872 | tf_op jit(solution)/shard_map/ppermute | solution.py:65
  62.6 11.0 %collective-permute-start.16 = (bf16[448,512]{1,0:T(8,128)(2,1)S(1)}, bf16[448,512]{1,0:T(8,128)(2,1)S(1)}, u32[]{:S(2)}, u32[]{:S(2)}) collective-permute-start(bf16[448,512]{1,0:T(8,128)(2,1)S(1)} %maximum_select_fusion.2.refs_0_), channel_id=1, source_target_pairs={{0,7},{1,0},{2,1},{3,2},{4,3},{5,4},{6,5},{7,6},{8,15},{9,8},{10,9... | collective-permute-start | bytes 1376264 | tf_op jit(solution)/shard_map/ppermute | solution.py:28
  62.6 12.0 %collective-permute-start.15 = (bf16[448,512]{1,0:T(8,128)(2,1)S(1)}, bf16[448,512]{1,0:T(8,128)(2,1)S(1)}, u32[]{:S(2)}, u32[]{:S(2)}) collective-permute-start(bf16[448,512]{1,0:T(8,128)(2,1)S(1)} %maximum_select_fusion.2.refs_0_), channel_id=1, source_target_pairs={{0,1},{1,2},{2,3},{3,4},{4,5},{5,6},{6,7},{7,0},{8,9},{9,10},{10,1... | collective-permute-start | bytes 1376264 | tf_op jit(solution)/shard_map/ppermute | solution.py:28
  64.7 6.1 %collective-permute-start.18 = (bf16[224,512]{1,0:T(8,128)(2,1)S(1)}, bf16[224,512]{1,0:T(8,128)(2,1)S(1)}, u32[]{:S(2)}, u32[]{:S(2)}) collective-permute-start(bf16[224,512]{1,0:T(8,128)(2,1)S(1)} %get-tuple-element.93), channel_id=1, source_target_pairs={{0,24},{1,25},{2,26},{3,27},{4,28},{5,29},{6,30},{7,31},{8,0},{9,1... | collective-permute-start | bytes 688136 | tf_op jit(solution)/shard_map/ppermute | solution.py:28
  64.8 8.5 %collective-permute-start.17 = (bf16[224,512]{1,0:T(8,128)(2,1)S(1)}, bf16[224,512]{1,0:T(8,128)(2,1)S(1)}, u32[]{:S(2)}, u32[]{:S(2)}) collective-permute-start(bf16[224,512]{1,0:T(8,128)(2,1)S(1)} %get-tuple-element.94), channel_id=1, source_target_pairs={{0,8},{1,9},{2,10},{3,11},{4,12},{5,13},{6,14},{7,15},{8,16},{9,17... | collective-permute-start | bytes 688136 | tf_op jit(solution)/shard_map/ppermute | solution.py:28
  74.6 6.6 %collective-permute-start.24 = (bf16[1024,512]{1,0:T(8,128)(2,1)S(1)}, bf16[1024,512]{1,0:T(8,128)(2,1)S(1)}, u32[]{:S(2)}, u32[]{:S(2)}) collective-permute-start(bf16[1024,512]{1,0:T(8,128)(2,1)S(1)} %pad_maximum_fusion.mine), channel_id=1, source_target_pairs={{0,32},{32,0},{64,96},{96,64},{128,160},{160,128},{192,224},{224,1... | collective-permute-start | bytes 3145736 | tf_op jit(solution)/shard_map/ppermute | solution.py:55
  74.6 14.1 %collective-permute-start.22 = (bf16[448,512]{1,0:T(8,128)(2,1)S(1)}, bf16[448,512]{1,0:T(8,128)(2,1)S(1)}, u32[]{:S(2)}, u32[]{:S(2)}) collective-permute-start(bf16[448,512]{1,0:T(8,128)(2,1)S(1)} %collective-permute-done.15.refs_1_), channel_id=1, source_target_pairs={{0,8},{1,9},{2,10},{3,11},{4,12},{5,13},{6,14},{7,15},{8,16},{9,17... | collective-permute-start | bytes 1376264 | tf_op jit(solution)/shard_map/ppermute | solution.py:28
  77.3 14.0 %collective-permute-start.20 = (bf16[448,512]{1,0:T(8,128)(2,1)S(1)}, bf16[448,512]{1,0:T(8,128)(2,1)}, u32[]{:S(2)}, u32[]{:S(2)}) collective-permute-start(bf16[448,512]{1,0:T(8,128)(2,1)S(1)} %collective-permute-done.15.refs_1_), channel_id=1, source_target_pairs={{0,1},{1,2},{2,3},{3,4},{4,5},{5,6},{6,7},{7,0},{8,9},{9,10},{10,1... | collective-permute-start | bytes 1376264 | tf_op jit(solution)/shard_map/ppermute | solution.py:28
  77.3 14.0 %collective-permute-start.23 = (bf16[448,512]{1,0:T(8,128)(2,1)S(1)}, bf16[448,512]{1,0:T(8,128)(2,1)S(1)}, u32[]{:S(2)}, u32[]{:S(2)}) collective-permute-start(bf16[448,512]{1,0:T(8,128)(2,1)S(1)} %collective-permute-done.16.refs_2_), channel_id=1, source_target_pairs={{0,24},{1,25},{2,26},{3,27},{4,28},{5,29},{6,30},{7,31},{8,0},{9,1... | collective-permute-start | bytes 1376264 | tf_op jit(solution)/shard_map/ppermute | solution.py:28
  79.2 12.1 %collective-permute-start.21 = (bf16[448,512]{1,0:T(8,128)(2,1)S(1)}, bf16[448,512]{1,0:T(8,128)(2,1)}, u32[]{:S(2)}, u32[]{:S(2)}) collective-permute-start(bf16[448,512]{1,0:T(8,128)(2,1)S(1)} %collective-permute-done.16.refs_2_), channel_id=1, source_target_pairs={{0,7},{1,0},{2,1},{3,2},{4,3},{5,4},{6,5},{7,6},{8,15},{9,8},{10,9... | collective-permute-start | bytes 1376264 | tf_op jit(solution)/shard_map/ppermute | solution.py:28
  91.3 41.4 %collective-permute-start.30 = (bf16[512,512]{1,0:T(8,128)(2,1)S(1)}, bf16[512,512]{1,0:T(8,128)(2,1)S(1)}, u32[]{:S(2)}, u32[]{:S(2)}) collective-permute-start(bf16[512,512]{1,0:T(8,128)(2,1)S(1)} %get-tuple-element.63), channel_id=1, source_target_pairs={{0,192},{32,224},{1,193},{33,225},{2,194},{34,226},{3,195},{35,227... | collective-permute-start | bytes 1572872 | tf_op jit(solution)/shard_map/ppermute | solution.py:42
  92.6 43.1 %collective-permute-start.29 = (bf16[512,512]{1,0:T(8,128)(2,1)S(1)}, bf16[512,512]{1,0:T(8,128)(2,1)S(1)}, u32[]{:S(2)}, u32[]{:S(2)}) collective-permute-start(bf16[512,512]{1,0:T(8,128)(2,1)S(1)} %get-tuple-element.63), channel_id=1, source_target_pairs={{0,64},{32,96},{1,65},{33,97},{2,66},{34,98},{3,67},{35,99},{4,68}... | collective-permute-start | bytes 1572872 | tf_op jit(solution)/shard_map/ppermute | solution.py:41
  93.3 42.5 %collective-permute-start.27 = (bf16[448,512]{1,0:T(8,128)(2,1)}, bf16[448,512]{1,0:T(8,128)(2,1)}, u32[]{:S(2)}, u32[]{:S(2)}) collective-permute-start(bf16[448,512]{1,0:T(8,128)(2,1)} %collective-permute-done.20.refs_3_), channel_id=1, source_target_pairs={{0,8},{1,9},{2,10},{3,11},{4,12},{5,13},{6,14},{7,15},{8,16},{9,17... | collective-permute-start | bytes 1376264 | tf_op jit(solution)/shard_map/ppermute | solution.py:28
  94.5 41.4 %collective-permute-start.25 = (bf16[448,512]{1,0:T(8,128)(2,1)}, bf16[448,512]{1,0:T(8,128)(2,1)S(1)}, u32[]{:S(2)}, u32[]{:S(2)}) collective-permute-start(bf16[448,512]{1,0:T(8,128)(2,1)} %collective-permute-done.20.refs_3_), channel_id=1, source_target_pairs={{0,1},{1,2},{2,3},{3,4},{4,5},{5,6},{6,7},{7,0},{8,9},{9,10},{10,1... | collective-permute-start | bytes 1376264 | tf_op jit(solution)/shard_map/ppermute | solution.py:28
  96.1 39.8 %collective-permute-start.28 = (bf16[448,512]{1,0:T(8,128)(2,1)}, bf16[448,512]{1,0:T(8,128)(2,1)}, u32[]{:S(2)}, u32[]{:S(2)}) collective-permute-start(bf16[448,512]{1,0:T(8,128)(2,1)} %collective-permute-done.21.refs_4_), channel_id=1, source_target_pairs={{0,24},{1,25},{2,26},{3,27},{4,28},{5,29},{6,30},{7,31},{8,0},{9,1... | collective-permute-start | bytes 1376264 | tf_op jit(solution)/shard_map/ppermute | solution.py:28
  132.7 11.5 %collective-permute-start.26 = (bf16[448,512]{1,0:T(8,128)(2,1)}, bf16[448,512]{1,0:T(8,128)(2,1)S(1)}, u32[]{:S(2)}, u32[]{:S(2)}) collective-permute-start(bf16[448,512]{1,0:T(8,128)(2,1)} %collective-permute-done.21.refs_4_), channel_id=1, source_target_pairs={{0,7},{1,0},{2,1},{3,2},{4,3},{5,4},{6,5},{7,6},{8,15},{9,8},{10,9... | collective-permute-start | bytes 1376264 | tf_op jit(solution)/shard_map/ppermute | solution.py:28
  144.2 9.0 %collective-permute-start.35 = (bf16[256,512]{1,0:T(8,128)(2,1)S(1)}, bf16[256,512]{1,0:T(8,128)(2,1)S(1)}, u32[]{:S(2)}, u32[]{:S(2)}) collective-permute-start(bf16[256,512]{1,0:T(8,128)(2,1)S(1)} %get-tuple-element.91), channel_id=1, source_target_pairs={{64,128},{96,160},{65,129},{97,161},{66,130},{98,162},{67,131},{99... | collective-permute-start | bytes 786440 | tf_op jit(solution)/shard_map/ppermute | solution.py:49
  144.8 8.3 %collective-permute-start.36 = (bf16[256,512]{1,0:T(8,128)(2,1)S(1)}, bf16[256,512]{1,0:T(8,128)(2,1)S(1)}, u32[]{:S(2)}, u32[]{:S(2)}) collective-permute-start(bf16[256,512]{1,0:T(8,128)(2,1)S(1)} %get-tuple-element.92), channel_id=1, source_target_pairs={{192,128},{224,160},{193,129},{225,161},{194,130},{226,162},{195,1... | collective-permute-start | bytes 786440 | tf_op jit(solution)/shard_map/ppermute | solution.py:50
  146.2 14.3 %collective-permute-start.33 = (bf16[448,512]{1,0:T(8,128)(2,1)S(1)}, bf16[448,512]{1,0:T(8,128)(2,1)S(1)}, u32[]{:S(2)}, u32[]{:S(2)}) collective-permute-start(bf16[448,512]{1,0:T(8,128)(2,1)S(1)} %collective-permute-done.25.refs_5_), channel_id=1, source_target_pairs={{0,8},{1,9},{2,10},{3,11},{4,12},{5,13},{6,14},{7,15},{8,16},{9,17... | collective-permute-start | bytes 1376264 | tf_op jit(solution)/shard_map/ppermute | solution.py:28
  147.2 13.2 %collective-permute-start.34 = (bf16[448,512]{1,0:T(8,128)(2,1)S(1)}, bf16[448,512]{1,0:T(8,128)(2,1)S(1)}, u32[]{:S(2)}, u32[]{:S(2)}) collective-permute-start(bf16[448,512]{1,0:T(8,128)(2,1)S(1)} %collective-permute-done.26.refs_6_), channel_id=1, source_target_pairs={{0,24},{1,25},{2,26},{3,27},{4,28},{5,29},{6,30},{7,31},{8,0},{9,1... | collective-permute-start | bytes 1376264 | tf_op jit(solution)/shard_map/ppermute | solution.py:28
  149.5 7.2 %collective-permute-start.32 = (bf16[224,512]{1,0:T(8,128)(2,1)S(1)}, bf16[224,512]{1,0:T(8,128)(2,1)S(1)}, u32[]{:S(2)}, u32[]{:S(2)}) collective-permute-start(bf16[224,512]{1,0:T(8,128)(2,1)S(1)} %slice.78), channel_id=1, source_target_pairs={{0,7},{1,0},{2,1},{3,2},{4,3},{5,4},{6,5},{7,6},{8,15},{9,8},{10,9... | collective-permute-start | bytes 688136 | tf_op jit(solution)/shard_map/ppermute | solution.py:28
  153.2 7.2 %collective-permute-start.31 = (bf16[224,512]{1,0:T(8,128)(2,1)S(1)}, bf16[224,512]{1,0:T(8,128)(2,1)S(1)}, u32[]{:S(2)}, u32[]{:S(2)}) collective-permute-start(bf16[224,512]{1,0:T(8,128)(2,1)S(1)} %slice.77), channel_id=1, source_target_pairs={{0,1},{1,2},{2,3},{3,4},{4,5},{5,6},{6,7},{7,0},{8,9},{9,10},{10,1... | collective-permute-start | bytes 688136 | tf_op jit(solution)/shard_map/ppermute | solution.py:28
  160.5 11.6 %collective-permute-start.38 = (bf16[224,512]{1,0:T(8,128)(2,1)S(1)}, bf16[224,512]{1,0:T(8,128)(2,1)S(1)}, u32[]{:S(2)}, u32[]{:S(2)}) collective-permute-start(bf16[224,512]{1,0:T(8,128)(2,1)S(1)} %collective-permute-done.31.refs_7_), channel_id=1, source_target_pairs={{0,8},{1,9},{2,10},{3,11},{4,12},{5,13},{6,14},{7,15},{8,16},{9,17... | collective-permute-start | bytes 688136 | tf_op jit(solution)/shard_map/ppermute | solution.py:28
  160.9 11.3 %collective-permute-start.39 = (bf16[224,512]{1,0:T(8,128)(2,1)S(1)}, bf16[224,512]{1,0:T(8,128)(2,1)S(1)}, u32[]{:S(2)}, u32[]{:S(2)}) collective-permute-start(bf16[224,512]{1,0:T(8,128)(2,1)S(1)} %collective-permute-done.32.refs_8_), channel_id=1, source_target_pairs={{0,24},{1,25},{2,26},{3,27},{4,28},{5,29},{6,30},{7,31},{8,0},{9,1... | collective-permute-start | bytes 688136 | tf_op jit(solution)/shard_map/ppermute | solution.py:28
  (28 other events, 303.0 us)

commit v2 on v1

--- a/solution.py
+++ b/solution.py
@@ -36,19 +36,12 @@
     return 2 * N * k + N * half if parity == 0 else 8 * N + 4 * N * half + N * k
 
 
-def beside_y(own):
+def along_y(own):
     y = lax.axis_index("prow") // 2
     ahead = lax.ppermute(own, "prow", [(0, 2), (1, 3)])
     back = lax.ppermute(own, "prow", [(0, 6), (1, 7)])
-    return jnp.where(y == 1, ahead, jnp.where(y == 3, back, own))
-
-
-def across_y(own):
-    y = lax.axis_index("prow") // 2
-    half = own.shape[0] // 2
-    low = lax.ppermute(own[:half], "prow", [(2, 4), (3, 5)])
-    high = lax.ppermute(own[half:], "prow", [(6, 4), (7, 5)])
-    return jnp.where(y == 2, jnp.concatenate([low, high], 0), own)
+    across = lax.ppermute(own, "prow", [(0, 4), (1, 5)])
+    return jnp.where(y == 0, own, jnp.where(y == 1, ahead, jnp.where(y == 2, across, back)))
 
 
 def swap_cores(value):
@@ -97,14 +90,12 @@
     single = choose(held[:N], *odd)
     both = choose(matrix[: 2 * N], *even)
     sent = jnp.where(x == 0, both, jnp.concatenate([single, single], 0))
-    sent, extra = tie(sent, extra)
     came = move(sent, [(node(a, c), node(b, c)) for a, b in ((0, 2), (1, 3), (3, 1)) for c in range(NZ)])
     extra = grow(extra, 1, x, z, core)
     first = jnp.where(x == 3, came[:N], sent[:N])
     second = jnp.where(x == 1, came[:N], sent[N:])
     double = jnp.where(x == 2, came, jnp.concatenate([first, second], 0))
 
-    double, extra = tie(double, extra)
     near_rows, far_rows = [(double, 0, 0, 0, 2)], []
     up = down = double
     xup, xdown = double[:N], double[N:]
@@ -119,11 +110,12 @@
             carried = (jnp.concatenate([block, grow(carried[0], 2, x, z, core)], 0),)
         elif s == 2:
             carried = make_weights(carried[0], swap_cores(carried[0]))
-        elif s == 3:
-            carried = (beside_y(carried[0]), carried[1])
-        else:
-            carried = (across_y(carried[0]), carried[1])
+        elif s == 4:
+            carried = (weights, top)
         up, down, xup, xdown, *carried = tie(up, down, xup, xdown, *carried)
+        if s == 2:
+            weights, top = along_y(carried[0]), carried[1]
+            carried = ()
         whole = 2 if 1 < s else 1
         far_rows.append((xup, 1, -dz, 0, whole))
         far_rows.append((xdown, 1, dz, 1 if s == 1 else 0, whole))

time: 182 us -> 171 us (0.940)
  the two profiles are of different devices: /device:TPU:152 before, /device:TPU:8 now
where the time goes in v2:
time: 171 us; the launch traced here: 169 us
  waiting for transfers between devices  79.9 us (47%)
  starting transfers between devices  55.8 us (33%)
  Pallas kernels  20 us (12%)
  local copies, waits for them, and re-layouts  9.08 us (5%)
  other arithmetic  3.4 us (2%)
    ppermute x27, starting transfers between devices, move(): return lax.ppermute(value, 'pcol', pairs)  48.1 us
    ppermute x27, waiting for transfers between devices, move(): return lax.ppermute(value, 'pcol', pairs)  45.7 us
    ppermute x1, waiting for transfers between devices, along_y(): ahead = lax.ppermute(own, 'prow', [(0, 2), (1, 3)])  34.2 us
    pallas_call x2, Pallas kernels, factor(): pl.pallas_call(functools.partial(factor_kernel, plan, part), out_shape=ja...  13.3 us
    pallas_call x1, Pallas kernels, make_weights(): pl.pallas_call(weights_kernel, out_shape=(jax.ShapeDtypeStruct((NB, NB),...  6.71 us
    ppermute x7, starting transfers between devices, send(): return lax.ppermute(value, ('prow', 'pcol'), pairs)  4.95 us
    unnamed x44, local copies, waits for them, and re-layouts  3.91 us
  transfers between devices with their start and end apart: 39, of which 9 were waited for; matrix products, arithmetic and copies ran while one was open for 3% of the time, Pallas kernels for 8%

profile of v2, /device:TPU:8, one launch (start us, length us, event | category | flops | bytes accessed | tf_op | source)
XLA Modules:
  0.0 169.1 jit_solution(9470716204420265368)
XLA Ops:
  0.0 2.4 %fusion.1 = (bf16[448,512]{1,0:T(8,128)(2,1)}, bf16[448,512]{1,0:T(8,128)(2,1)}, bf16[448,512]{1,0:T(8,128)(2,1)}) fusion(bf16[3584,512]{1,0:T(8,128)(2,1)} %a_hbm.3), kind=kLoop, calls=%fused_computation.13 | loop fusion | bytes 2752512 | tf_op jit(solution)/shard_map/slice | solution.py:74
  2.4 1.6 fusion
  4.0 4.7 %collective-permute-start.1 = (bf16[896,512]{1,0:T(8,128)(2,1)S(1)}, bf16[896,512]{1,0:T(8,128)(2,1)S(1)}, u32[]{:S(2)}, u32[]{:S(2)}) collective-permute-start(bf16[896,512]{1,0:T(8,128)(2,1)S(1)} %get-tuple-element.69), channel_id=1, source_target_pairs={{0,24},{1,25},{32,56},{33,57},{64,88},{65,89},{96,120},{97,121},{1... | collective-permute-start | bytes 2752520 | tf_op jit(solution)/shard_map/ppermute | solution.py:28
  8.7 2.3 %collective-permute-start = (bf16[896,512]{1,0:T(8,128)(2,1)S(1)}, bf16[896,512]{1,0:T(8,128)(2,1)}, u32[]{:S(2)}, u32[]{:S(2)}) collective-permute-start(bf16[896,512]{1,0:T(8,128)(2,1)S(1)} %get-tuple-element.70), channel_id=1, source_target_pairs={{0,8},{1,9},{32,40},{33,41},{64,72},{65,73},{96,104},{97,105},{128... | collective-permute-start | bytes 2752520 | tf_op jit(solution)/shard_map/ppermute | solution.py:28
  11.0 3.9 %collective-permute-start.2 = (bf16[448,512]{1,0:T(8,128)(2,1)}, bf16[448,512]{1,0:T(8,128)(2,1)}, u32[]{:S(2)}, u32[]{:S(2)}) collective-permute-start(bf16[448,512]{1,0:T(8,128)(2,1)} %get-tuple-element.38), channel_id=1, source_target_pairs={{0,7},{1,2},{32,39},{33,34},{64,71},{65,66},{96,103},{97,98},{128,... | collective-permute-start | bytes 1376264 | tf_op jit(solution)/shard_map/ppermute | solution.py:28
  14.9 2.1 %collective-permute-start.3 = (bf16[448,512]{1,0:T(8,128)(2,1)}, bf16[448,512]{1,0:T(8,128)(2,1)}, u32[]{:S(2)}, u32[]{:S(2)}) collective-permute-start(bf16[448,512]{1,0:T(8,128)(2,1)} %get-tuple-element.39), channel_id=1, source_target_pairs={{0,6},{1,3},{32,38},{33,35},{64,70},{65,67},{96,102},{97,99},{128,... | collective-permute-start | bytes 1376264 | tf_op jit(solution)/shard_map/ppermute | solution.py:28
  17.0 2.1 %collective-permute-start.4 = (bf16[448,512]{1,0:T(8,128)(2,1)}, bf16[448,512]{1,0:T(8,128)(2,1)}, u32[]{:S(2)}, u32[]{:S(2)}) collective-permute-start(bf16[448,512]{1,0:T(8,128)(2,1)} %get-tuple-element.40), channel_id=1, source_target_pairs={{0,5},{1,4},{32,37},{33,36},{64,69},{65,68},{96,101},{97,100},{128... | collective-permute-start | bytes 1376264 | tf_op jit(solution)/shard_map/ppermute | solution.py:28
  20.1 5.2 %collective-permute-done.2 = bf16[448,512]{1,0:T(8,128)(2,1)} collective-permute-done((bf16[448,512]{1,0:T(8,128)(2,1)}, bf16[448,512]{1,0:T(8,128)(2,1)}, u32[]{:S(2)}, u32[]{:S(2)}) %collective-permute-start.2) | collective-permute-done | bytes 458784 | tf_op jit(solution)/shard_map/ppermute | solution.py:28
  26.0 9.1 %collective-permute-done.3 = bf16[448,512]{1,0:T(8,128)(2,1)} collective-permute-done((bf16[448,512]{1,0:T(8,128)(2,1)}, bf16[448,512]{1,0:T(8,128)(2,1)}, u32[]{:S(2)}, u32[]{:S(2)}) %collective-permute-start.3) | collective-permute-done | bytes 458784 | tf_op jit(solution)/shard_map/ppermute | solution.py:28
  35.9 8.0 %collective-permute-done.4 = bf16[448,512]{1,0:T(8,128)(2,1)} collective-permute-done((bf16[448,512]{1,0:T(8,128)(2,1)}, bf16[448,512]{1,0:T(8,128)(2,1)}, u32[]{:S(2)}, u32[]{:S(2)}) %collective-permute-start.4) | collective-permute-done | bytes 458784 | tf_op jit(solution)/shard_map/ppermute | solution.py:28
  46.8 1.2 select_select_fusion.2
  50.2 1.5 maximum_select_fusion
  51.7 1.3 collective-permute-start.8
  54.0 8.1 %collective-permute-done.8 = bf16[448,512]{1,0:T(8,128)(2,1)S(1)} collective-permute-done((bf16[448,512]{1,0:T(8,128)(2,1)S(1)}, bf16[448,512]{1,0:T(8,128)(2,1)S(1)}, u32[]{:S(2)}, u32[]{:S(2)}) %collective-permute-start.8) | collective-permute-done | bytes 458784 | tf_op jit(solution)/shard_map/ppermute | solution.py:28
  62.4 2.0 %collective-permute-start.9 = (bf16[448,512]{1,0:T(8,128)(2,1)S(1)}, bf16[448,512]{1,0:T(8,128)(2,1)S(1)}, u32[]{:S(2)}, u32[]{:S(2)}) collective-permute-start(bf16[448,512]{1,0:T(8,128)(2,1)S(1)} %maximum_select_fusion.1.refs_0_), channel_id=1, source_target_pairs={{0,1},{1,2},{2,3},{3,4},{4,5},{5,6},{6,7},{7,0},{8,9},{9,10},{10,1... | collective-permute-start | bytes 1376264 | tf_op jit(solution)/shard_map/ppermute | solution.py:28
  64.5 3.7 %collective-permute-start.12 = (bf16[224,512]{1,0:T(8,128)(2,1)S(1)}, bf16[224,512]{1,0:T(8,128)(2,1)S(1)}, u32[]{:S(2)}, u32[]{:S(2)}) collective-permute-start(bf16[224,512]{1,0:T(8,128)(2,1)S(1)} %get-tuple-element.79), channel_id=1, source_target_pairs={{0,24},{1,25},{2,26},{3,27},{4,28},{5,29},{6,30},{7,31},{8,0},{9,1... | collective-permute-start | bytes 688136 | tf_op jit(solution)/shard_map/ppermute | solution.py:28
  69.0 3.8 %collective-permute-done.12.refs_1_ = bf16[224,512]{1,0:T(8,128)(2,1)S(1)} collective-permute-done((bf16[224,512]{1,0:T(8,128)(2,1)S(1)}, bf16[224,512]{1,0:T(8,128)(2,1)S(1)}, u32[]{:S(2)}, u32[]{:S(2)}) %collective-permute-start.12) | collective-permute-done | bytes 229408 | tf_op jit(solution)/shard_map/ppermute | solution.py:28
  72.8 2.7 %collective-permute-done.11.refs_0_ = bf16[224,512]{1,0:T(8,128)(2,1)S(1)} collective-permute-done((bf16[224,512]{1,0:T(8,128)(2,1)S(1)}, bf16[224,512]{1,0:T(8,128)(2,1)S(1)}, u32[]{:S(2)}, u32[]{:S(2)}) %collective-permute-start.11) | collective-permute-done | bytes 229408 | tf_op jit(solution)/shard_map/ppermute | solution.py:28
  76.2 3.4 %collective-permute-start.22 = (bf16[448,512]{1,0:T(8,128)(2,1)S(1)}, bf16[448,512]{1,0:T(8,128)(2,1)S(1)}, u32[]{:S(2)}, u32[]{:S(2)}) collective-permute-start(bf16[448,512]{1,0:T(8,128)(2,1)S(1)} %collective-permute-done.9.refs_1_), channel_id=1, source_target_pairs={{0,8},{1,9},{2,10},{3,11},{4,12},{5,13},{6,14},{7,15},{8,16},{9,17... | collective-permute-start | bytes 1376264 | tf_op jit(solution)/shard_map/ppermute | solution.py:28
  80.2 2.6 %collective-permute-start.21 = (bf16[448,512]{1,0:T(8,128)(2,1)S(1)}, bf16[448,512]{1,0:T(8,128)(2,1)S(1)}, u32[]{:S(2)}, u32[]{:S(2)}) collective-permute-start(bf16[448,512]{1,0:T(8,128)(2,1)S(1)} %collective-permute-done.10.refs_2_), channel_id=1, source_target_pairs={{0,7},{1,0},{2,1},{3,2},{4,3},{5,4},{6,5},{7,6},{8,15},{9,8},{10,9... | collective-permute-start | bytes 1376264 | tf_op jit(solution)/shard_map/ppermute | solution.py:28
  82.9 6.7 %shard_map.37 = (bf16[512,512]{1,0:T(8,128)(2,1)S(1)}, bf16[512,512]{1,0:T(8,128)(2,1)S(1)}) custom-call(s32[2]{0:T(128)S(1)} %pad_add_fusion.ids, bf16[1024,512]{1,0:T(8,128)(2,1)S(1)} %pad_maximum_fusion.mine, bf16[1024,512]{1,0:T(8,128)(2,1)S(1)} %collective-permute-done.24.other, f32[2,512,512]{2,1,0:T(8,128)S(1)} %copy-done.2, f32[2,512,512]{2,1,0:T(8,128)} %l.1), custom_call_target="tpu_custom_call" | custom-call | flops 4563402752 | bytes 4194304 | tf_op jit(solution)/shard_map/pallas_call | solution.py:175
  90.5 2.9 %collective-permute-done.20.refs_3_ = bf16[448,512]{1,0:T(8,128)(2,1)S(1)} collective-permute-done((bf16[448,512]{1,0:T(8,128)(2,1)S(1)}, bf16[448,512]{1,0:T(8,128)(2,1)S(1)}, u32[]{:S(2)}, u32[]{:S(2)}) %collective-permute-start.20) | collective-permute-done | bytes 458784 | tf_op jit(solution)/shard_map/ppermute | solution.py:28
  94.4 3.1 %collective-permute-start.28 = (bf16[448,512]{1,0:T(8,128)(2,1)S(1)}, bf16[448,512]{1,0:T(8,128)(2,1)S(1)}, u32[]{:S(2)}, u32[]{:S(2)}) collective-permute-start(bf16[448,512]{1,0:T(8,128)(2,1)S(1)} %collective-permute-done.21.refs_4_), channel_id=1, source_target_pairs={{0,24},{1,25},{2,26},{3,27},{4,28},{5,29},{6,30},{7,31},{8,0},{9,1... | collective-permute-start | bytes 1376264 | tf_op jit(solution)/shard_map/ppermute | solution.py:28
  97.5 2.5 %collective-permute-start.26 = (bf16[448,512]{1,0:T(8,128)(2,1)S(1)}, bf16[448,512]{1,0:T(8,128)(2,1)S(1)}, u32[]{:S(2)}, u32[]{:S(2)}) collective-permute-start(bf16[448,512]{1,0:T(8,128)(2,1)S(1)} %collective-permute-done.21.refs_4_), channel_id=1, source_target_pairs={{0,7},{1,0},{2,1},{3,2},{4,3},{5,4},{6,5},{7,6},{8,15},{9,8},{10,9... | collective-permute-start | bytes 1376264 | tf_op jit(solution)/shard_map/ppermute | solution.py:28
  100.7 5.8 %collective-permute-done.27.refs_4_ = bf16[448,512]{1,0:T(8,128)(2,1)S(1)} collective-permute-done((bf16[448,512]{1,0:T(8,128)(2,1)S(1)}, bf16[448,512]{1,0:T(8,128)(2,1)S(1)}, u32[]{:S(2)}, u32[]{:S(2)}) %collective-permute-start.27) | collective-permute-done | bytes 458784 | tf_op jit(solution)/shard_map/ppermute | solution.py:28
  107.2 1.3 collective-permute-start.33
  109.3 2.6 %collective-permute-start.32 = (bf16[448,512]{1,0:T(8,128)(2,1)S(1)}, bf16[448,512]{1,0:T(8,128)(2,1)}, u32[]{:S(2)}, u32[]{:S(2)}) collective-permute-start(bf16[448,512]{1,0:T(8,128)(2,1)S(1)} %collective-permute-done.26.refs_6_), channel_id=1, source_target_pairs={{0,24},{1,25},{2,26},{3,27},{4,28},{5,29},{6,30},{7,31},{8,0},{9,1... | collective-permute-start | bytes 1376264 | tf_op jit(solution)/shard_map/ppermute | solution.py:28
  111.9 3.6 %collective-permute-start.30 = (bf16[224,512]{1,0:T(8,128)(2,1)S(1)}, bf16[224,512]{1,0:T(8,128)(2,1)S(1)}, u32[]{:S(2)}, u32[]{:S(2)}) collective-permute-start(bf16[224,512]{1,0:T(8,128)(2,1)S(1)} %slice.72), channel_id=1, source_target_pairs={{0,7},{1,0},{2,1},{3,2},{4,3},{5,4},{6,5},{7,6},{8,15},{9,8},{10,9... | collective-permute-start | bytes 688136 | tf_op jit(solution)/shard_map/ppermute | solution.py:28
  115.5 34.2 %collective-permute-done.33 = bf16[512,512]{1,0:T(8,128)(2,1)S(1)} collective-permute-done((bf16[512,512]{1,0:T(8,128)(2,1)S(1)}, bf16[512,512]{1,0:T(8,128)(2,1)S(1)}, u32[]{:S(2)}, u32[]{:S(2)}) %collective-permute-start.33) | collective-permute-done | bytes 524320 | tf_op jit(solution)/shard_map/ppermute | solution.py:41
  150.1 3.2 %collective-permute-start.38 = (bf16[224,512]{1,0:T(8,128)(2,1)S(1)}, bf16[224,512]{1,0:T(8,128)(2,1)S(1)}, u32[]{:S(2)}, u32[]{:S(2)}) collective-permute-start(bf16[224,512]{1,0:T(8,128)(2,1)S(1)} %collective-permute-done.30.refs_8_), channel_id=1, source_target_pairs={{0,24},{1,25},{2,26},{3,27},{4,28},{5,29},{6,30},{7,31},{8,0},{9,1... | collective-permute-start | bytes 688136 | tf_op jit(solution)/shard_map/ppermute | solution.py:28
  154.1 6.6 %shard_map.38.refs_10_ = bf16[3584,512]{1,0:T(8,128)(2,1)} custom-call(s32[2]{0:T(128)} %copy-done.1, bf16[3584,512]{1,0:T(8,128)(2,1)} %a_hbm.3, bf16[512,512]{1,0:T(8,128)(2,1)} %copy-done.3, bf16[512,512]{1,0:T(8,128)(2,1)} %copy-done.5, bf16[512,512]{1,0:T(8,128)(2,1)} %copy-done, bf16[448,512]{1,0:T(8,128)(2,1)} %copy-done.4, ...), custom_call_target="tpu_custom_call" | custom-call | flops 1879048192 | bytes 7340032 | tf_op jit(solution)/shard_map/pallas_call | solution.py:261
  162.1 6.8 %shard_map.39 = bf16[3584,512]{1,0:T(8,128)(2,1)} custom-call(s32[2]{0:T(128)} %copy-done.1, bf16[3584,512]{1,0:T(8,128)(2,1)} %a_hbm.3, bf16[512,512]{1,0:T(8,128)(2,1)} %copy-done.3, bf16[512,512]{1,0:T(8,128)(2,1)} %copy-done.5, bf16[512,512]{1,0:T(8,128)(2,1)} %copy-done, bf16[224,512]{1,0:T(8,128)(2,1)} %copy-done.17, ...), custom_call_target="tpu_custom_call", output_to_operand_aliasing={{}: (15, {})} | custom-call | flops 1879048192 | bytes 7340032 | tf_op jit(solution)/shard_map/pallas_call | solution.py:261
  (111 shorter events, 17.3 us)
Async XLA Ops:
  4.0 40.6 %collective-permute-start.1 = (bf16[896,512]{1,0:T(8,128)(2,1)S(1)}, bf16[896,512]{1,0:T(8,128)(2,1)S(1)}, u32[]{:S(2)}, u32[]{:S(2)}) collective-permute-start(bf16[896,512]{1,0:T(8,128)(2,1)S(1)} %get-tuple-element.69), channel_id=1, source_target_pairs={{0,24},{1,25},{32,56},{33,57},{64,88},{65,89},{96,120},{97,121},{1... | collective-permute-start | bytes 2752520 | tf_op jit(solution)/shard_map/ppermute | solution.py:28
  8.7 35.9 %collective-permute-start = (bf16[896,512]{1,0:T(8,128)(2,1)S(1)}, bf16[896,512]{1,0:T(8,128)(2,1)}, u32[]{:S(2)}, u32[]{:S(2)}) collective-permute-start(bf16[896,512]{1,0:T(8,128)(2,1)S(1)} %get-tuple-element.70), channel_id=1, source_target_pairs={{0,8},{1,9},{32,40},{33,41},{64,72},{65,73},{96,104},{97,105},{128... | collective-permute-start | bytes 2752520 | tf_op jit(solution)/shard_map/ppermute | solution.py:28
  11.0 14.3 %collective-permute-start.2 = (bf16[448,512]{1,0:T(8,128)(2,1)}, bf16[448,512]{1,0:T(8,128)(2,1)}, u32[]{:S(2)}, u32[]{:S(2)}) collective-permute-start(bf16[448,512]{1,0:T(8,128)(2,1)} %get-tuple-element.38), channel_id=1, source_target_pairs={{0,7},{1,2},{32,39},{33,34},{64,71},{65,66},{96,103},{97,98},{128,... | collective-permute-start | bytes 1376264 | tf_op jit(solution)/shard_map/ppermute | solution.py:28
  14.9 20.3 %collective-permute-start.3 = (bf16[448,512]{1,0:T(8,128)(2,1)}, bf16[448,512]{1,0:T(8,128)(2,1)}, u32[]{:S(2)}, u32[]{:S(2)}) collective-permute-start(bf16[448,512]{1,0:T(8,128)(2,1)} %get-tuple-element.39), channel_id=1, source_target_pairs={{0,6},{1,3},{32,38},{33,35},{64,70},{65,67},{96,102},{97,99},{128,... | collective-permute-start | bytes 1376264 | tf_op jit(solution)/shard_map/ppermute | solution.py:28
  17.0 26.9 %collective-permute-start.4 = (bf16[448,512]{1,0:T(8,128)(2,1)}, bf16[448,512]{1,0:T(8,128)(2,1)}, u32[]{:S(2)}, u32[]{:S(2)}) collective-permute-start(bf16[448,512]{1,0:T(8,128)(2,1)} %get-tuple-element.40), channel_id=1, source_target_pairs={{0,5},{1,4},{32,37},{33,36},{64,69},{65,68},{96,101},{97,100},{128... | collective-permute-start | bytes 1376264 | tf_op jit(solution)/shard_map/ppermute | solution.py:28
  25.3 20.8 %collective-permute-start.15 = (bf16[512,512]{1,0:T(8,128)(2,1)S(1)}, bf16[512,512]{1,0:T(8,128)(2,1)S(1)}, u32[]{:S(2)}, u32[]{:S(2)}) collective-permute-start(bf16[512,512]{1,0:T(8,128)(2,1)S(1)} %slice.70), channel_id=1, source_target_pairs={{1,5},{32,36}} | collective-permute-start | bytes 1572872 | tf_op jit(solution)/shard_map/ppermute | solution.py:58
  35.2 11.6 %collective-permute-start.14 = (bf16[512,512]{1,0:T(8,128)(2,1)S(1)}, bf16[512,512]{1,0:T(8,128)(2,1)S(1)}, u32[]{:S(2)}, u32[]{:S(2)}) collective-permute-start(bf16[512,512]{1,0:T(8,128)(2,1)S(1)} %slice.70), channel_id=1, source_target_pairs={{1,7},{32,38}} | collective-permute-start | bytes 1572872 | tf_op jit(solution)/shard_map/ppermute | solution.py:58
  48.0 5.0 %collective-permute-start.18 = (bf16[512,512]{1,0:T(8,128)(2,1)S(1)}, bf16[512,512]{1,0:T(8,128)(2,1)S(1)}, u32[]{:S(2)}, u32[]{:S(2)}) collective-permute-start(bf16[512,512]{1,0:T(8,128)(2,1)S(1)} %select_select_fusion.2), channel_id=1, source_target_pairs={{1,17},{3,19},{5,21},{7,23},{32,48},{34,50},{36,52},{38,54}} | collective-permute-start | bytes 1572872 | tf_op jit(solution)/shard_map/ppermute | solution.py:58
  51.7 10.5 %collective-permute-start.8 = (bf16[448,512]{1,0:T(8,128)(2,1)S(1)}, bf16[448,512]{1,0:T(8,128)(2,1)S(1)}, u32[]{:S(2)}, u32[]{:S(2)}) collective-permute-start(bf16[448,512]{1,0:T(8,128)(2,1)S(1)} %maximum_select_fusion), channel_id=1, source_target_pairs={{0,16},{1,17},{2,18},{3,19},{4,20},{5,21},{6,22},{7,23},{8,24},{9,... | collective-permute-start | bytes 1376264 | tf_op jit(solution)/shard_map/ppermute | solution.py:28
  53.2 15.7 %collective-permute-start.19 = (bf16[512,512]{1,0:T(8,128)(2,1)S(1)}, bf16[512,512]{1,0:T(8,128)(2,1)S(1)}, u32[]{:S(2)}, u32[]{:S(2)}) collective-permute-start(bf16[512,512]{1,0:T(8,128)(2,1)S(1)} %select_select_fusion.1), channel_id=1, source_target_pairs={{1,2},{3,4},{5,6},{7,0},{9,10},{11,12},{13,14},{15,8},{17,18},{19,... | collective-permute-start | bytes 1572872 | tf_op jit(solution)/shard_map/ppermute | solution.py:58
  62.4 13.1 %collective-permute-start.10 = (bf16[448,512]{1,0:T(8,128)(2,1)S(1)}, bf16[448,512]{1,0:T(8,128)(2,1)S(1)}, u32[]{:S(2)}, u32[]{:S(2)}) collective-permute-start(bf16[448,512]{1,0:T(8,128)(2,1)S(1)} %maximum_select_fusion.1.refs_0_), channel_id=1, source_target_pairs={{0,7},{1,0},{2,1},{3,2},{4,3},{5,4},{6,5},{7,6},{8,15},{9,8},{10,9... | collective-permute-start | bytes 1376264 | tf_op jit(solution)/shard_map/ppermute | solution.py:28
  62.4 13.0 %collective-permute-start.9 = (bf16[448,512]{1,0:T(8,128)(2,1)S(1)}, bf16[448,512]{1,0:T(8,128)(2,1)S(1)}, u32[]{:S(2)}, u32[]{:S(2)}) collective-permute-start(bf16[448,512]{1,0:T(8,128)(2,1)S(1)} %maximum_select_fusion.1.refs_0_), channel_id=1, source_target_pairs={{0,1},{1,2},{2,3},{3,4},{4,5},{5,6},{6,7},{7,0},{8,9},{9,10},{10,1... | collective-permute-start | bytes 1376264 | tf_op jit(solution)/shard_map/ppermute | solution.py:28
  64.5 8.3 %collective-permute-start.12 = (bf16[224,512]{1,0:T(8,128)(2,1)S(1)}, bf16[224,512]{1,0:T(8,128)(2,1)S(1)}, u32[]{:S(2)}, u32[]{:S(2)}) collective-permute-start(bf16[224,512]{1,0:T(8,128)(2,1)S(1)} %get-tuple-element.79), channel_id=1, source_target_pairs={{0,24},{1,25},{2,26},{3,27},{4,28},{5,29},{6,30},{7,31},{8,0},{9,1... | collective-permute-start | bytes 688136 | tf_op jit(solution)/shard_map/ppermute | solution.py:28
  68.2 7.2 %collective-permute-start.11 = (bf16[224,512]{1,0:T(8,128)(2,1)S(1)}, bf16[224,512]{1,0:T(8,128)(2,1)S(1)}, u32[]{:S(2)}, u32[]{:S(2)}) collective-permute-start(bf16[224,512]{1,0:T(8,128)(2,1)S(1)} %get-tuple-element.80), channel_id=1, source_target_pairs={{0,8},{1,9},{2,10},{3,11},{4,12},{5,13},{6,14},{7,15},{8,16},{9,17... | collective-permute-start | bytes 688136 | tf_op jit(solution)/shard_map/ppermute | solution.py:28
  76.2 6.7 %collective-permute-start.24 = (bf16[1024,512]{1,0:T(8,128)(2,1)S(1)}, bf16[1024,512]{1,0:T(8,128)(2,1)S(1)}, u32[]{:S(2)}, u32[]{:S(2)}) collective-permute-start(bf16[1024,512]{1,0:T(8,128)(2,1)S(1)} %pad_maximum_fusion.mine), channel_id=1, source_target_pairs={{0,32},{32,0},{64,96},{96,64},{128,160},{160,128},{192,224},{224,1... | collective-permute-start | bytes 3145736 | tf_op jit(solution)/shard_map/ppermute | solution.py:48
  76.2 14.3 %collective-permute-start.22 = (bf16[448,512]{1,0:T(8,128)(2,1)S(1)}, bf16[448,512]{1,0:T(8,128)(2,1)S(1)}, u32[]{:S(2)}, u32[]{:S(2)}) collective-permute-start(bf16[448,512]{1,0:T(8,128)(2,1)S(1)} %collective-permute-done.9.refs_1_), channel_id=1, source_target_pairs={{0,8},{1,9},{2,10},{3,11},{4,12},{5,13},{6,14},{7,15},{8,16},{9,17... | collective-permute-start | bytes 1376264 | tf_op jit(solution)/shard_map/ppermute | solution.py:28
  79.6 13.8 %collective-permute-start.20 = (bf16[448,512]{1,0:T(8,128)(2,1)S(1)}, bf16[448,512]{1,0:T(8,128)(2,1)S(1)}, u32[]{:S(2)}, u32[]{:S(2)}) collective-permute-start(bf16[448,512]{1,0:T(8,128)(2,1)S(1)} %collective-permute-done.9.refs_1_), channel_id=1, source_target_pairs={{0,1},{1,2},{2,3},{3,4},{4,5},{5,6},{6,7},{7,0},{8,9},{9,10},{10,1... | collective-permute-start | bytes 1376264 | tf_op jit(solution)/shard_map/ppermute | solution.py:28
  79.6 13.8 %collective-permute-start.23 = (bf16[448,512]{1,0:T(8,128)(2,1)S(1)}, bf16[448,512]{1,0:T(8,128)(2,1)S(1)}, u32[]{:S(2)}, u32[]{:S(2)}) collective-permute-start(bf16[448,512]{1,0:T(8,128)(2,1)S(1)} %collective-permute-done.10.refs_2_), channel_id=1, source_target_pairs={{0,24},{1,25},{2,26},{3,27},{4,28},{5,29},{6,30},{7,31},{8,0},{9,1... | collective-permute-start | bytes 1376264 | tf_op jit(solution)/shard_map/ppermute | solution.py:28
  80.2 13.2 %collective-permute-start.21 = (bf16[448,512]{1,0:T(8,128)(2,1)S(1)}, bf16[448,512]{1,0:T(8,128)(2,1)S(1)}, u32[]{:S(2)}, u32[]{:S(2)}) collective-permute-start(bf16[448,512]{1,0:T(8,128)(2,1)S(1)} %collective-permute-done.10.refs_2_), channel_id=1, source_target_pairs={{0,7},{1,0},{2,1},{3,2},{4,3},{5,4},{6,5},{7,6},{8,15},{9,8},{10,9... | collective-permute-start | bytes 1376264 | tf_op jit(solution)/shard_map/ppermute | solution.py:28
  93.4 13.0 %collective-permute-start.27 = (bf16[448,512]{1,0:T(8,128)(2,1)S(1)}, bf16[448,512]{1,0:T(8,128)(2,1)S(1)}, u32[]{:S(2)}, u32[]{:S(2)}) collective-permute-start(bf16[448,512]{1,0:T(8,128)(2,1)S(1)} %collective-permute-done.20.refs_3_), channel_id=1, source_target_pairs={{0,8},{1,9},{2,10},{3,11},{4,12},{5,13},{6,14},{7,15},{8,16},{9,17... | collective-permute-start | bytes 1376264 | tf_op jit(solution)/shard_map/ppermute | solution.py:28
  94.4 12.8 %collective-permute-start.25 = (bf16[448,512]{1,0:T(8,128)(2,1)S(1)}, bf16[448,512]{1,0:T(8,128)(2,1)S(1)}, u32[]{:S(2)}, u32[]{:S(2)}) collective-permute-start(bf16[448,512]{1,0:T(8,128)(2,1)S(1)} %collective-permute-done.20.refs_3_), channel_id=1, source_target_pairs={{0,1},{1,2},{2,3},{3,4},{4,5},{5,6},{6,7},{7,0},{8,9},{9,10},{10,1... | collective-permute-start | bytes 1376264 | tf_op jit(solution)/shard_map/ppermute | solution.py:28
  94.4 14.1 %collective-permute-start.28 = (bf16[448,512]{1,0:T(8,128)(2,1)S(1)}, bf16[448,512]{1,0:T(8,128)(2,1)S(1)}, u32[]{:S(2)}, u32[]{:S(2)}) collective-permute-start(bf16[448,512]{1,0:T(8,128)(2,1)S(1)} %collective-permute-done.21.refs_4_), channel_id=1, source_target_pairs={{0,24},{1,25},{2,26},{3,27},{4,28},{5,29},{6,30},{7,31},{8,0},{9,1... | collective-permute-start | bytes 1376264 | tf_op jit(solution)/shard_map/ppermute | solution.py:28
  97.5 11.0 %collective-permute-start.26 = (bf16[448,512]{1,0:T(8,128)(2,1)S(1)}, bf16[448,512]{1,0:T(8,128)(2,1)S(1)}, u32[]{:S(2)}, u32[]{:S(2)}) collective-permute-start(bf16[448,512]{1,0:T(8,128)(2,1)S(1)} %collective-permute-done.21.refs_4_), channel_id=1, source_target_pairs={{0,7},{1,0},{2,1},{3,2},{4,3},{5,4},{6,5},{7,6},{8,15},{9,8},{10,9... | collective-permute-start | bytes 1376264 | tf_op jit(solution)/shard_map/ppermute | solution.py:28
  100.0 11.9 %collective-permute-start.35 = (bf16[512,512]{1,0:T(8,128)(2,1)S(1)}, bf16[512,512]{1,0:T(8,128)(2,1)S(1)}, u32[]{:S(2)}, u32[]{:S(2)}) collective-permute-start(bf16[512,512]{1,0:T(8,128)(2,1)S(1)} %get-tuple-element.55), channel_id=1, source_target_pairs={{0,192},{32,224},{1,193},{33,225},{2,194},{34,226},{3,195},{35,227... | collective-permute-start | bytes 1572872 | tf_op jit(solution)/shard_map/ppermute | solution.py:42
  106.5 9.0 %collective-permute-start.34 = (bf16[512,512]{1,0:T(8,128)(2,1)S(1)}, bf16[512,512]{1,0:T(8,128)(2,1)S(1)}, u32[]{:S(2)}, u32[]{:S(2)}) collective-permute-start(bf16[512,512]{1,0:T(8,128)(2,1)S(1)} %get-tuple-element.55), channel_id=1, source_target_pairs={{0,128},{32,160},{1,129},{33,161},{2,130},{34,162},{3,131},{35,163... | collective-permute-start | bytes 1572872 | tf_op jit(solution)/shard_map/ppermute | solution.py:43
  107.2 42.5 %collective-permute-start.33 = (bf16[512,512]{1,0:T(8,128)(2,1)S(1)}, bf16[512,512]{1,0:T(8,128)(2,1)S(1)}, u32[]{:S(2)}, u32[]{:S(2)}) collective-permute-start(bf16[512,512]{1,0:T(8,128)(2,1)S(1)} %get-tuple-element.55), channel_id=1, source_target_pairs={{0,64},{32,96},{1,65},{33,97},{2,66},{34,98},{3,67},{35,99},{4,68}... | collective-permute-start | bytes 1572872 | tf_op jit(solution)/shard_map/ppermute | solution.py:41
  108.5 41.3 %collective-permute-start.31 = (bf16[448,512]{1,0:T(8,128)(2,1)S(1)}, bf16[448,512]{1,0:T(8,128)(2,1)}, u32[]{:S(2)}, u32[]{:S(2)}) collective-permute-start(bf16[448,512]{1,0:T(8,128)(2,1)S(1)} %collective-permute-done.25.refs_5_), channel_id=1, source_target_pairs={{0,8},{1,9},{2,10},{3,11},{4,12},{5,13},{6,14},{7,15},{8,16},{9,17... | collective-permute-start | bytes 1376264 | tf_op jit(solution)/shard_map/ppermute | solution.py:28
  109.3 40.6 %collective-permute-start.32 = (bf16[448,512]{1,0:T(8,128)(2,1)S(1)}, bf16[448,512]{1,0:T(8,128)(2,1)}, u32[]{:S(2)}, u32[]{:S(2)}) collective-permute-start(bf16[448,512]{1,0:T(8,128)(2,1)S(1)} %collective-permute-done.26.refs_6_), channel_id=1, source_target_pairs={{0,24},{1,25},{2,26},{3,27},{4,28},{5,29},{6,30},{7,31},{8,0},{9,1... | collective-permute-start | bytes 1376264 | tf_op jit(solution)/shard_map/ppermute | solution.py:28
  111.9 37.9 %collective-permute-start.30 = (bf16[224,512]{1,0:T(8,128)(2,1)S(1)}, bf16[224,512]{1,0:T(8,128)(2,1)S(1)}, u32[]{:S(2)}, u32[]{:S(2)}) collective-permute-start(bf16[224,512]{1,0:T(8,128)(2,1)S(1)} %slice.72), channel_id=1, source_target_pairs={{0,7},{1,0},{2,1},{3,2},{4,3},{5,4},{6,5},{7,6},{8,15},{9,8},{10,9... | collective-permute-start | bytes 688136 | tf_op jit(solution)/shard_map/ppermute | solution.py:28
  115.5 34.4 %collective-permute-start.29 = (bf16[224,512]{1,0:T(8,128)(2,1)S(1)}, bf16[224,512]{1,0:T(8,128)(2,1)S(1)}, u32[]{:S(2)}, u32[]{:S(2)}) collective-permute-start(bf16[224,512]{1,0:T(8,128)(2,1)S(1)} %slice.71), channel_id=1, source_target_pairs={{0,1},{1,2},{2,3},{3,4},{4,5},{5,6},{6,7},{7,0},{8,9},{9,10},{10,1... | collective-permute-start | bytes 688136 | tf_op jit(solution)/shard_map/ppermute | solution.py:28
  150.0 10.7 %collective-permute-start.37 = (bf16[224,512]{1,0:T(8,128)(2,1)S(1)}, bf16[224,512]{1,0:T(8,128)(2,1)S(1)}, u32[]{:S(2)}, u32[]{:S(2)}) collective-permute-start(bf16[224,512]{1,0:T(8,128)(2,1)S(1)} %collective-permute-done.29.refs_7_), channel_id=1, source_target_pairs={{0,8},{1,9},{2,10},{3,11},{4,12},{5,13},{6,14},{7,15},{8,16},{9,17... | collective-permute-start | bytes 688136 | tf_op jit(solution)/shard_map/ppermute | solution.py:28
  150.1 10.7 %collective-permute-start.38 = (bf16[224,512]{1,0:T(8,128)(2,1)S(1)}, bf16[224,512]{1,0:T(8,128)(2,1)S(1)}, u32[]{:S(2)}, u32[]{:S(2)}) collective-permute-start(bf16[224,512]{1,0:T(8,128)(2,1)S(1)} %collective-permute-done.30.refs_8_), channel_id=1, source_target_pairs={{0,24},{1,25},{2,26},{3,27},{4,28},{5,29},{6,30},{7,31},{8,0},{9,1... | collective-permute-start | bytes 688136 | tf_op jit(solution)/shard_map/ppermute | solution.py:28
  (29 other events, 322.0 us)
